TPU v7x, 32 devices: a whole 2x2x4 slice. The times are simulated.
32 devices in a mesh: batch: 16 (over z, y, x), tower: 2 (over core).
Axes of the slice: x: 2, y: 2, z: 4, core: 2. Of those that a mesh axis runs over, the one named last changes fastest.
Arguments:
- crop_pixels: bfloat16 [512, 13, 13, 384], P(('batch', 'tower')), may hold values from -6 to 6
- live_rows: int32 [32], P(('batch', 'tower')), may hold values from 1 to 16, 256 in all
- conv_weight: bfloat16 [2, 3, 3, 384, 256], replicated, may hold values from -0.109375 to 0.109375
- conv_bias: float32 [2, 256], replicated, may hold values from -3 to 3
- stitch_conv: float32 [2, 2, 256], replicated, may hold values from 0.2 to 1
- fc_weight: bfloat16 [2, 9216, 4096], P('tower', 'batch'), may hold values from -0.25 to 0.25
- fc_bias: float32 [2, 4096], P('tower'), may hold values from -3 to 3
- stitch_fc: float32 [2, 2, 4096], replicated, may hold values from 0.2 to 1
- cotangent: bfloat16 [2, 512, 4096], P('tower', 'batch'), may hold values from -6 to 6
Outputs:
- stitched_out: bfloat16 [2, 512, 4096], P('tower', 'batch')
- d_crops: bfloat16 [512, 13, 13, 384], P(('batch', 'tower'))
- d_conv_weight: float32 [2, 3, 3, 384, 256], replicated
- d_conv_bias: float32 [2, 256], replicated
- d_stitch_conv: float32 [2, 2, 256], replicated
- d_fc_weight: float32 [2, 9216, 4096], P('tower', 'batch')
- d_fc_bias: float32 [2, 4096], replicated
- d_stitch_fc: float32 [2, 2, 4096], replicated
Inputs may be any that keep to these rules, and one draw needn't show every extreme that they name: Each device's first live_rows slots hold crops, the others are padding; the counts add up to half of all 512 slots, and some device has all 16 slots live.
All inputs are finite; a program needn't handle non-finite values.
Results may differ from a plain program's by a relative error of at most 0.0073.
Values may be sent and summed in bfloat16 or wider, within the bound.
A program may use at most 384 MiB of HBM per device.

v0:
```python
import jax
import jax.numpy as jnp
from jax import lax
from jax.sharding import PartitionSpec as P


def from_partner(block, axis, distance):
    count = lax.axis_size(axis)
    route = []
    for low in range(count):
        high = low | 1 << distance
        if high != low and high < count:
            route += [(low, high), (high, low)]
    return lax.ppermute(block, axis, route)


def shards(
    crop_pixels,
    live_rows,
    conv_weight,
    conv_bias,
    stitch_conv,
    fc_weight,
    fc_bias,
    stitch_fc,
    cotangent,
):
    slots = crop_pixels.shape[0]
    extent = crop_pixels.shape[1]
    in_chan = crop_pixels.shape[3]
    out_chan = conv_weight.shape[4]
    pooled_side = (extent - 3) // 2 + 1
    span = 2 * pooled_side - 1
    feature_count = pooled_side * pooled_side * out_chan
    spatial = slots * extent * extent
    taps = conv_weight.transpose(1, 2, 3, 0, 4).reshape(3, 3, in_chan, 2 * out_chan)
    padded = jnp.pad(crop_pixels, ((0, 0), (1, 1), (1, 1), (0, 0)))
    preact = jnp.zeros((spatial, 2 * out_chan), jnp.float32)
    for row_tap in range(3):
        for col_tap in range(3):
            window = padded[:, row_tap : row_tap + extent, col_tap : col_tap + extent, :].reshape(
                spatial, in_chan
            )
            preact = preact + jnp.dot(
                window, taps[row_tap, col_tap], preferred_element_type=jnp.float32
            )
    preact = (preact + conv_bias.reshape(1, 2 * out_chan)).reshape(
        slots, extent, extent, 2, out_chan
    )
    activated, gelu_conv_back = jax.vjp(jax.nn.gelu, preact)
    pooled = jnp.zeros((slots, pooled_side, pooled_side, 2, out_chan), jnp.float32)
    for row_tap in range(3):
        for col_tap in range(3):
            pooled = (
                pooled + activated[:, row_tap : row_tap + span : 2, col_tap : col_tap + span : 2]
            )
    pooled = pooled / 9.0
    mixed = jnp.stack(
        [
            stitch_conv[tower_id, 0] * pooled[:, :, :, 0]
            + stitch_conv[tower_id, 1] * pooled[:, :, :, 1]
            for tower_id in range(2)
        ],
        axis=1,
    )
    features = mixed.reshape(slots, 2, feature_count).astype(jnp.bfloat16)
    count_pair = jnp.broadcast_to(live_rows.reshape(1, 1), (1, 2))
    pair_rows, pair_counts = (
        lax.all_to_all(features, "tower", split_axis=1, concat_axis=0, tiled=True),
        lax.all_to_all(count_pair, "tower", split_axis=1, concat_axis=0, tiled=True),
    )
    pair_features = pair_rows.reshape(2 * slots, feature_count)
    tower_index = lax.axis_index("tower")
    slot_index = jnp.arange(2 * slots, dtype=jnp.int32)
    live_here = jnp.where(slot_index // slots == 0, pair_counts[0, 0], pair_counts[1, 0])
    alive_rows = (slot_index % slots < live_here).astype(jnp.float32)[:, None]
    columns = pair_features
    hidden = jnp.dot(
        columns,
        lax.all_gather(fc_weight, "batch", axis=1, tiled=True)[0],
        preferred_element_type=jnp.float32,
    )
    hidden = hidden + fc_bias[0][None, :]
    gate_value, gelu_fc_back = jax.vjp(jax.nn.gelu, hidden)
    gate_low = gate_value.astype(jnp.bfloat16)
    partner_gate = from_partner(gate_low, "tower", 0)
    first_tower = tower_index == 0
    own_weight = jnp.where(first_tower, stitch_fc[0, 0], stitch_fc[1, 1])
    cross_weight = jnp.where(first_tower, stitch_fc[0, 1], stitch_fc[1, 0])
    back_weight = jnp.where(first_tower, stitch_fc[1, 0], stitch_fc[0, 1])
    own_gate = gate_low.astype(jnp.float32)
    other_gate = partner_gate.astype(jnp.float32)
    stitched = (own_weight[None, :] * own_gate + cross_weight[None, :] * other_gate) * alive_rows
    stitched_out = stitched.astype(jnp.bfloat16)[None]
    partner_cot = from_partner(cotangent[0], "tower", 0)
    own_grad = cotangent[0].astype(jnp.float32) * alive_rows
    other_grad = partner_cot.astype(jnp.float32) * alive_rows
    d_own_mix = jnp.sum(own_grad * own_gate, axis=0)
    d_cross_mix = jnp.sum(own_grad * other_gate, axis=0)
    d_gate = own_weight[None, :] * own_grad + back_weight[None, :] * other_grad
    d_hidden = gelu_fc_back(d_gate)[0].astype(jnp.bfloat16)
    d_fc_row = jnp.sum(d_hidden.astype(jnp.float32), axis=0)
    columns = pair_features
    d_fc_weight = lax.psum_scatter(
        lax.dot_general(
            columns, d_hidden, (((0,), (0,)), ((), ())), preferred_element_type=jnp.float32
        ),
        "batch",
        scatter_dimension=0,
        tiled=True,
    )[None]
    d_rows = lax.dot_general(
        d_hidden,
        lax.all_gather(fc_weight, "batch", axis=1, tiled=True)[0],
        (((1,), (1,)), ((), ())),
        preferred_element_type=jnp.float32,
    )
    d_rows = d_rows.astype(jnp.bfloat16).reshape(2 * slots, 1, feature_count)
    d_features = lax.all_to_all(d_rows, "tower", split_axis=0, concat_axis=1, tiled=True)
    d_mixed = d_features.astype(jnp.float32).reshape(slots, 2, pooled_side, pooled_side, out_chan)
    d_stitch_conv = jnp.stack(
        [
            jnp.stack(
                [
                    jnp.sum(d_mixed[:, tower_id] * pooled[:, :, :, source], axis=(0, 1, 2))
                    for source in range(2)
                ],
                axis=0,
            )
            for tower_id in range(2)
        ],
        axis=0,
    )
    d_pooled = (
        jnp.stack(
            [
                stitch_conv[0, source] * d_mixed[:, 0] + stitch_conv[1, source] * d_mixed[:, 1]
                for source in range(2)
            ],
            axis=3,
        )
        / 9.0
    )
    d_activated = jnp.zeros((slots, extent, extent, 2, out_chan), jnp.float32)
    for row_tap in range(3):
        for col_tap in range(3):
            d_activated = d_activated.at[
                :, row_tap : row_tap + span : 2, col_tap : col_tap + span : 2
            ].add(d_pooled)
    d_preact = (
        gelu_conv_back(d_activated)[0]
        .astype(jnp.bfloat16)
        .reshape(slots, extent, extent, 2 * out_chan)
    )
    d_flat = d_preact.reshape(spatial, 2 * out_chan)
    d_conv_bias = jnp.sum(d_flat.astype(jnp.float32), axis=0).reshape(2, out_chan)
    padded_grad = jnp.pad(d_preact, ((0, 0), (1, 1), (1, 1), (0, 0)))
    d_pixels = jnp.zeros((spatial, in_chan), jnp.float32)
    tap_grads = []
    for row_tap in range(3):
        for col_tap in range(3):
            window = padded[:, row_tap : row_tap + extent, col_tap : col_tap + extent, :].reshape(
                spatial, in_chan
            )
            tap_grads.append(
                lax.dot_general(
                    window, d_flat, (((0,), (0,)), ((), ())), preferred_element_type=jnp.float32
                )
            )
            moved = padded_grad[
                :, 2 - row_tap : 2 - row_tap + extent, 2 - col_tap : 2 - col_tap + extent, :
            ].reshape(spatial, 2 * out_chan)
            d_pixels = d_pixels + lax.dot_general(
                moved,
                taps[row_tap, col_tap],
                (((1,), (1,)), ((), ())),
                preferred_element_type=jnp.float32,
            )
    d_crops = d_pixels.reshape(slots, extent, extent, in_chan).astype(jnp.bfloat16)
    d_kernel = (
        jnp.stack(tap_grads, axis=0).reshape(3, 3, in_chan, 2, out_chan).transpose(3, 0, 1, 2, 4)
    )
    tower_rows = jnp.arange(2, dtype=jnp.int32)[:, None]
    d_fc_bias = jnp.where(tower_rows == tower_index, d_fc_row[None, :], 0.0)
    mix_first = jnp.where(first_tower, jnp.stack([d_own_mix, d_cross_mix], axis=0), 0.0)
    mix_second = jnp.where(first_tower, 0.0, jnp.stack([d_cross_mix, d_own_mix], axis=0))
    d_stitch_fc = jnp.stack([mix_first, mix_second], axis=0)
    d_kernel, d_conv_bias, d_stitch_conv, d_fc_bias, d_stitch_fc = lax.psum(
        (d_kernel, d_conv_bias, d_stitch_conv, d_fc_bias, d_stitch_fc), ("batch", "tower")
    )
    return (
        stitched_out,
        d_crops,
        d_kernel,
        d_conv_bias,
        d_stitch_conv,
        d_fc_weight,
        d_fc_bias,
        d_stitch_fc,
    )


def solution(mesh):
    in_specs = (
        P(("batch", "tower"), None, None, None),
        P(("batch", "tower")),
        P(),
        P(),
        P(),
        P("tower", "batch", None),
        P("tower", None),
        P(),
        P("tower", "batch", None),
    )
    out_specs = (
        P("tower", "batch", None),
        P(("batch", "tower"), None, None, None),
        P(),
        P(),
        P(),
        P("tower", "batch", None),
        P(),
        P(),
    )
    return jax.shard_map(shards, mesh=mesh, in_specs=in_specs, out_specs=out_specs, check_vma=False)
```

profile of v0, /device:TPU:1, one launch (start us, length us, event | category | flops | bytes accessed | tf_op | source)
XLA Modules:
  0.0 3201.1 jit_solution(15580898348713264848)
XLA Ops:
  9.1 3.8 all-to-all-start.1
  20.0 5.0 copy.128
  25.1 12.8 pad_slice_fusion.8
  39.9 4.7 reshape.451
  48.2 4.7 reshape.444
  56.5 4.7 reshape.445
  64.8 4.7 reshape.446
  69.6 3.6 copy.133
  73.2 4.7 reshape.448
  77.9 3.6 copy.134
  81.5 4.7 reshape.449
  86.2 3.6 copy.135
  89.8 4.7 reshape.450
  98.1 4.9 reshape.442
  103.1 5.7 fusion.53
  108.8 4.1 fusion.49
  112.9 4.1 fusion.56
  117.0 4.1 fusion.55
  121.2 4.2 fusion.54
  125.4 4.0 fusion.52
  129.4 4.2 fusion.51
  133.6 4.1 fusion.50
  137.7 22.2 add_add_fusion
  159.9 7.6 reshape.452
  175.2 3.8 all-to-all-start
  183.8 576.6 %all-gather.2.cloned.1.call-done = bf16[1,9216,4096]{2,1,0:T(8,128)(2,1)} async-done(((bf16[1,576,4096]{2,1,0:T(8,128)(2,1)}), bf16[1,9216,4096]{2,1,0:T(8,128)(2,1)}) %all-gather.2.cloned.1.call-update) | async-done | bytes 75497488 | tf_op jit(solution)/shard_map/all_gather | solution.py:80
  760.4 29.4 convert_reduce_fusion.1
  789.8 29.7 fusion.7
  822.3 4.6 all-to-all-start.2
  834.4 7.4 scatter_fusion
  841.7 7.4 scatter_fusion.1
  849.1 7.4 scatter_fusion.2
  856.4 7.4 scatter_fusion.3
  863.8 7.4 scatter_fusion.4
  871.2 7.4 scatter_fusion.5
  878.5 7.4 scatter_fusion.6
  885.9 7.4 scatter_fusion.7
  893.2 7.4 scatter_fusion.8
  900.6 7.4 convert_reduce_fusion
  931.8 9.8 reshape.465
  941.6 6.8 copy.198
  951.4 53.1 %fusion.70 = f32[9216,4096]{1,0:T(8,128)} fusion(bf16[32,9216]{1,0:T(8,128)(2,1)S(1)} %bitcast.282, bf16[32,4096]{1,0:T(8,128)(2,1)} %copy-done.33), kind=kOutput, calls=%fused_computation.176 | convolution fusion | flops 2415919104 | bytes 151846912 | tf_op jit(solution)/shard_map/dot_general | solution.py:105
  1004.8 6.8 pad_slice_fusion
  1048.2 5.2 copy.161
  1053.4 5.9 reshape.456
  1085.8 39.8 %all-reduce.2 = (f32[2,256]{1,0:T(2,128)}, f32[2,2,256]{2,1,0:T(2,128)}, f32[2,4096]{1,0:T(2,128)}) all-reduce(f32[2,256]{1,0:T(2,128)S(1)} %copy-done.42, f32[2,2,256]{2,1,0:T(2,128)S(1)} %pad_maximum_fusion.2, f32[2,4096]{1,0:T(2,128)S(1)} %broadcast_select_fusion), channel_id=1, replica_groups=mesh['batch'=16,'tower'=2] {'batch','tower'}, use_global_device_ids=true, to_apply=%region_11.12 | all-reduce | flops 9728 | bytes 77824 | tf_op jit(solution)/shard_map/psum | solution.py:188
  1125.5 2061.4 %reduce-scatter.2.cloned.1.call-done = f32[576,4096]{1,0:T(8,128)} async-done(((f32[9216,4096]{1,0:T(8,128)}), f32[576,4096]{1,0:T(8,128)}) %reduce-scatter.2.cloned.1.call-update) | async-done | bytes 9437200 | tf_op jit(solution)/shard_map/reduce_scatter | solution.py:104
  3186.9 6.6 copy.221
  (208 shorter events, 137.7 us)
Async XLA Ops:
  7.2 5.9 copy-start.44
  7.2 6.5 copy-start.43
  7.2 753.2 %all-gather.2.cloned.1.call-start = ((), (), s32[]{:S(2)}) async-start(), calls=%async_computation.4 | async-start | bytes 80216064 | tf_op jit(solution)/shard_map/all_gather | solution.py:80
  9.1 166.0 %all-to-all-start.1 = ((s32[1,2,1]{2,0,1:T(1,128)}), s32[1,2,1]{2,0,1:T(1,128)}, u32[]{:S(2)}, u32[]{:S(2)}) async-start(s32[1,2,1]{2,0,1:T(1,128)} %broadcast_in_dim.112), calls=%async_computation.1 | async-start | bytes 2048 | tf_op jit(solution)/shard_map/all_to_all | solution.py:70
  13.0 170.8 %collective-permute-start.1 = (bf16[32,4096]{1,0:T(8,128)(2,1)}, bf16[32,4096]{1,0:T(8,128)(2,1)}, u32[]{:S(2)}, u32[]{:S(2)}) collective-permute-start(bf16[32,4096]{1,0:T(8,128)(2,1)} %bitcast.27), channel_id=1, source_target_pairs={{0,1},{1,0},{2,3},{3,2},{4,5},{5,4},{6,7},{7,6},{8,9},{9,8},{10,11... | collective-permute-start | bytes 786440 | tf_op jit(solution)/shard_map/ppermute | solution.py:14
  25.1 112.7 %copy-start = (bf16[2,3,3,384,256]{3,4,0,2,1:T(8,128)(2,1)}, bf16[2,3,3,384,256]{3,4,0,2,1:T(8,128)(2,1)S(1)}, u32[]{:S(2)}) copy-start(bf16[2,3,3,384,256]{3,4,0,2,1:T(8,128)(2,1)S(1)} %copy.128) | copy-start | bytes 10616836
  103.1 5.8 copy-start.24
  108.8 4.1 copy-start.22
  112.9 4.1 copy-start.18
  117.0 4.1 copy-start.14
  121.1 4.2 copy-start.20
  125.4 4.0 copy-start.16
  129.4 4.2 copy-start.12
  172.9 1.2 copy-start.34
  172.9 1.2 copy-start.35
  173.8 6.6 copy-start.38
  173.8 586.6 %copy-start.41 = (f32[1,4096]{1,0:T(1,128)S(1)}, f32[1,4096]{1,0:T(1,128)}, u32[]{:S(2)}) copy-start(f32[1,4096]{1,0:T(1,128)} %param.15) | copy-start | bytes 49156
  175.2 8.6 all-to-all-start
  789.8 29.7 copy-start.33
  822.3 6.0 all-to-all-start.2
  826.9 298.7 %all-reduce.6.cloned.1.call-start = ((), (), s32[]{:S(2)}) async-start(), calls=%async_computation.6 | async-start | bytes 14286848 | tf_op jit(solution)/shard_map/psum | solution.py:188
  826.9 121.6 %collective-permute-start = (bf16[32,4096]{1,0:T(8,128)(2,1)}, bf16[32,4096]{1,0:T(8,128)(2,1)}, u32[]{:S(2)}, u32[]{:S(2)}) collective-permute-start(bf16[32,4096]{1,0:T(8,128)(2,1)} %get-tuple-element.82), channel_id=1, source_target_pairs={{0,1},{1,0},{2,3},{3,2},{4,5},{5,4},{6,7},{7,6},{8,9},{9,8},{10,11... | collective-permute-start | bytes 786440 | tf_op jit(solution)/shard_map/ppermute | solution.py:14
  910.2 1.8 copy-start.25
  910.7 18.9 copy-start.3
  912.0 2.2 copy-start.13
  914.2 2.2 copy-start.17
  916.4 2.2 copy-start.21
  918.6 2.2 copy-start.11
  920.8 2.2 copy-start.15
  923.0 2.2 copy-start.19
  925.2 2.2 copy-start.23
  927.4 2.2 copy-start.28
  951.3 2235.6 %reduce-scatter.2.cloned.1.call-start = ((), (), s32[]{:S(2)}) async-start(), calls=%async_computation.5 | async-start | bytes 160432128 | tf_op jit(solution)/shard_map/reduce_scatter | solution.py:104
  1053.4 6.0 copy-start.1
  1059.4 3.6 copy-start.5
  1063.0 1.8 copy-start.7
  1064.8 1.8 copy-start.9
  1066.6 1.8 copy-start.4
  1068.3 1.8 copy-start.6
  1070.1 1.8 copy-start.8
  1071.9 1.8 copy-start.10
  1073.7 2.0 copy-start.2
  1082.3 1.9 copy-start.27
  1082.3 1.9 copy-start.30
  1082.3 2.6 copy-start.32
  1082.4 3.3 copy-start.40
  1082.4 3.4 copy-start.42
  3186.9 6.6 copy-start.39
  (5 other events, 5.5 us)
Sparse Core Ops, SparseCore 0:
  10.9 749.4 all-gather.1
  951.4 164.5 all-reduce.5
  1123.6 2063.2 reduce-scatter.1
where the time goes:
time: 3210 us; the launch traced here: 3200 us
  waiting for transfers between devices  2640 us (82%)
  matrix products  207 us (6%)
  local copies, waits for them, and re-layouts  199 us (6%)
  other arithmetic  86.8 us (3%)
  blocking collectives  39.8 us (1%)
    reduce_scatter x1, waiting for transfers between devices, shards(): lax.psum_scatter(lax.dot_general(columns, d_hidden, (((0,), (0,)), ((), (...  2060 us
    all_gather x1, waiting for transfers between devices, shards(): lax.all_gather(fc_weight, 'batch', axis=1, tiled=True)[0]  577 us
    scatter-add x9, other arithmetic, shards(): d_activated = d_activated.at[:, row_tap:row_tap + span:2, col_tap:col_tap...  66.2 us
  transfers between devices with their start and end apart: 8, of which 3 were waited for; matrix products, arithmetic and copies ran while one was open for 13% of the time, Pallas kernels for 0%

commit v1 on v0

v1 whole, which is shorter than its diff:
```python
import functools, math
import jax, jax.numpy as jnp
from jax import lax
from jax.experimental import pallas as pl
from jax.experimental.pallas import tpu as pltpu
from jax.sharding import PartitionSpec as P
F32, BF16 = jnp.float32, jnp.bfloat16
CG = math.sqrt(2.0 / math.pi)

def gelu_pair(v):
    sq = v * v
    t = jnp.tanh(v * (CG + (CG * 0.044715) * sq))
    half = 0.5 + 0.5 * t
    value = v * half
    slope = half + value * (1.0 - half) * (2.0 * CG + (6.0 * CG * 0.044715) * sq)
    return value, slope

def conv_fwd_kernel(rows_per, x_ref, w_ref, b_ref, mix_ref, feat_ref, pooled_ref, slope_ref, p_ref, stage, act, fbuf):
    slots, side, _, cin = x_ref.shape
    towers, _, cout = w_ref.shape
    pool = (side - 3) // 2 + 1
    pitch = 16
    lanes = cin // 128
    p_ref[0] = jnp.zeros(p_ref.shape[1:], BF16)
    p_ref[side + 1] = jnp.zeros(p_ref.shape[1:], BF16)
    def put(k, _):
        r = k // side
        i = k % side
        v = x_ref[r, i].astype(F32)
        for l in range(lanes):
            stage[l, pl.ds(pl.multiple_of(k * pitch, pitch), side), :] = v[:, l * 128:(l + 1) * 128]
        return 0
    lax.fori_loop(0, slots * side, put, 0, unroll=4)
    def take(i, _):
        p_ref[i + 1, 0] = jnp.zeros((slots, cin), BF16)
        p_ref[i + 1, side + 1] = jnp.zeros((slots, cin), BF16)
        for j in range(side):
            for l in range(lanes):
                v = stage[l, pl.ds(i * pitch + j, slots, stride=side * pitch), :]
                p_ref[i + 1, j + 1, :, l * 128:(l + 1) * 128] = v.astype(BF16)
        return 0
    lax.fori_loop(0, side, take, 0)
    rows = rows_per * side * slots
    def row(y):
        window = jnp.concatenate(
            [p_ref[pl.ds(y + a, rows_per), b:b + side].reshape(rows, cin) for a in range(3) for b in range(3)], axis=1)
        for t in range(towers):
            pre = jnp.dot(window, w_ref[t], preferred_element_type=F32) + b_ref[t][None]
            value, slope = gelu_pair(pre)
            act[pl.ds(y, rows_per), :, :, t * cout:(t + 1) * cout] = value.reshape(rows_per, side, slots, cout)
            slope_ref[pl.ds(y, rows_per), :, :, t * cout:(t + 1) * cout] = slope.astype(BF16).reshape(rows_per, side, slots, cout)
    lax.fori_loop(0, side // rows_per, lambda k, _: (row(k * rows_per), 0)[1], 0)
    for i in range(pool):
        s3 = act[2 * i] + act[2 * i + 1] + act[2 * i + 2]
        for j in range(pool):
            p9 = (s3[2 * j] + s3[2 * j + 1] + s3[2 * j + 2]) * (1.0 / 9.0)
            pooled_ref[i * pool + j] = p9
            for t in range(towers):
                m = mix_ref[t, 0][None] * p9[:, :cout] + mix_ref[t, 1][None] * p9[:, cout:]
                fbuf[t, :, (i * pool + j) * cout:(i * pool + j + 1) * cout] = m.astype(BF16)
    nb, per = feat_ref.shape[1], feat_ref.shape[3]
    for t in range(towers):
        for b in range(nb):
            feat_ref[t, b] = fbuf[t, :, b * per:(b + 1) * per]

def conv_fwd(x, w, bias, mix, nb, rows_per=1):
    slots, side, _, cin = x.shape
    towers, _, _, _, cout = w.shape
    pool = (side - 3) // 2 + 1
    nf = pool * pool * cout
    V = pl.BlockSpec(memory_space=pltpu.VMEM)
    return pl.pallas_call(
        functools.partial(conv_fwd_kernel, rows_per),
        out_shape=[jax.ShapeDtypeStruct((towers, nb, slots, nf // nb), BF16),
                   jax.ShapeDtypeStruct((pool * pool, slots, towers * cout), F32),
                   jax.ShapeDtypeStruct((side, side, slots, towers * cout), BF16),
                   jax.ShapeDtypeStruct((side + 2, side + 2, slots, cin), BF16)],
        in_specs=[V] * 4, out_specs=[V] * 4,
        scratch_shapes=[pltpu.VMEM((cin // 128, slots * side * 16, 128), F32),
                        pltpu.VMEM((side, side, slots, towers * cout), F32),
                        pltpu.VMEM((towers, slots, nf), BF16)],
        compiler_params=pltpu.CompilerParams(vmem_limit_bytes=60 * 2**20),
    )(x, w.reshape(towers, 9 * cin, cout), bias, mix)

def conv_bwd_kernel(dm_ref, pooled_ref, slope_ref, p_ref, w_ref, mix_ref, dx_ref, dw_ref, small_ref,
                    fbuf, z, dpad, d2, dt, stage):
    towers, nb, slots, per = dm_ref.shape
    side = slope_ref.shape[0]
    cout = w_ref.shape[2]
    cin = p_ref.shape[3]
    pool = (side - 3) // 2 + 1
    wide = towers * cout
    cells = side * side
    for t in range(towers):
        for b in range(nb):
            fbuf[t, :, b * per:(b + 1) * per] = dm_ref[t, b]
    z[0] = jnp.zeros(z.shape[1:], F32)
    z[pool + 1] = jnp.zeros(z.shape[1:], F32)
    acc = [[jnp.zeros((slots, cout), F32)] * 2 for _ in range(2)]
    for i in range(pool):
        z[i + 1, 0] = jnp.zeros(z.shape[2:], F32)
        z[i + 1, pool + 1] = jnp.zeros(z.shape[2:], F32)
        for j in range(pool):
            q = i * pool + j
            dm = [fbuf[t, :, q * cout:(q + 1) * cout].astype(F32) for t in range(towers)]
            for u in range(towers):
                pu = pooled_ref[q, :, u * cout:(u + 1) * cout]
                for t in range(towers):
                    acc[t][u] = acc[t][u] + dm[t] * pu
                z[i + 1, j + 1, :, u * cout:(u + 1) * cout] = (mix_ref[0, u][None] * dm[0] + mix_ref[1, u][None] * dm[1]) * (1.0 / 9.0)
    dpad[0] = jnp.zeros(dpad.shape[1:], BF16)
    dpad[side + 1] = jnp.zeros(dpad.shape[1:], BF16)
    d2[cells:] = jnp.zeros((d2.shape[0] - cells, slots, wide), BF16)
    def drow(y, src):
        dpad[y + 1, 0] = jnp.zeros((slots, wide), BF16)
        dpad[y + 1, side + 1] = jnp.zeros((slots, wide), BF16)
        for x in range(side):
            j = x // 2
            v = src(j + 1) if x % 2 else src(j) + src(j + 1)
            d = (v * slope_ref[y, x].astype(F32)).astype(BF16)
            dpad[y + 1, x + 1] = d
            d2[y * side + x] = d
    def pair(i, _):
        drow(2 * i, lambda j: z[i, j] + z[i + 1, j])
        drow(2 * i + 1, lambda j: z[i + 1, j])
        return 0
    lax.fori_loop(0, pool, pair, 0)
    drow(side - 1, lambda j: z[pool, j] + z[pool + 1, j])
    step = 256 // slots
    def flip(k, _):
        dt[:, pl.ds(pl.multiple_of(k * 256, 256), 256)] = d2[pl.ds(k * step, step)].reshape(256, wide).T
        return 0
    lax.fori_loop(0, d2.shape[0] // step, flip, 0)
    tail = (d2.shape[0] - cells) * slots
    for a in range(3):
        win = jnp.concatenate([p_ref[a:a + side, b:b + side].reshape(cells * slots, cin) for b in range(3)], axis=1)
        win = jnp.concatenate([win, jnp.zeros((tail, 3 * cin), BF16)], axis=0)
        dw_ref[a] = jnp.dot(dt[...], win, preferred_element_type=F32)
    ones = jnp.ones((d2.shape[0] * slots, 128), BF16)
    small_ref[:, 0:128] = jnp.dot(dt[...], ones, preferred_element_type=F32)
    rows = jnp.concatenate([jnp.concatenate([jnp.sum(acc[t][u], axis=0, keepdims=True) for u in range(2)], axis=1) for t in range(2)], axis=0)
    small_ref[:, 128:256] = jnp.concatenate([rows, jnp.zeros((126, wide), F32)], axis=0).T
    pitch = 16
    def xrow(y):
        lhs = jnp.concatenate([dpad[y + 2 - a, 2 - b:2 - b + side, :, t * cout:(t + 1) * cout].reshape(side * slots, cout)
                               for t in range(towers) for a in range(3) for b in range(3)], axis=1)
        rhs = jnp.concatenate([w_ref[t, (a * 3 + b) * cin:(a * 3 + b + 1) * cin, :]
                               for t in range(towers) for a in range(3) for b in range(3)], axis=1)
        out = lax.dot_general(lhs, rhs, (((1,), (1,)), ((), ())), preferred_element_type=F32).reshape(side, slots, cin)
        for x in range(side):
            for l in range(cin // 128):
                stage[l, pl.ds(y * pitch + x, slots, stride=side * pitch), :] = out[x, :, l * 128:(l + 1) * 128]
    lax.fori_loop(0, side, lambda y, _: (xrow(y), 0)[1], 0)
    def put(k, _):
        r = k // side
        i = k % side
        dx_ref[r, i] = jnp.concatenate([stage[l, pl.ds(pl.multiple_of(k * pitch, pitch), side), :] for l in range(cin // 128)], axis=1).astype(BF16)
        return 0
    lax.fori_loop(0, slots * side, put, 0, unroll=4)

def conv_bwd(dm, pooled, slope, p, w, mix):
    towers, nb, slots, per = dm.shape
    side = slope.shape[0]
    cin = p.shape[3]
    cout = w.shape[4]
    pool = (side - 3) // 2 + 1
    wide = towers * cout
    V = pl.BlockSpec(memory_space=pltpu.VMEM)
    cells = -(-side * side * slots // 256) * 256 // slots
    return pl.pallas_call(
        conv_bwd_kernel,
        out_shape=[jax.ShapeDtypeStruct((slots, side, side, cin), BF16),
                   jax.ShapeDtypeStruct((3, wide, 3 * cin), F32),
                   jax.ShapeDtypeStruct((wide, 256), F32)],
        in_specs=[V] * 6, out_specs=[V] * 3,
        scratch_shapes=[pltpu.VMEM((towers, slots, nb * per), BF16),
                        pltpu.VMEM((pool + 2, pool + 2, slots, wide), F32),
                        pltpu.VMEM((side + 2, side + 2, slots, wide), BF16),
                        pltpu.VMEM((cells, slots, wide), BF16),
                        pltpu.VMEM((wide, cells * slots), BF16),
                        pltpu.VMEM((cin // 128, slots * side * 16, 128), F32)],
        compiler_params=pltpu.CompilerParams(vmem_limit_bytes=62 * 2**20),
    )(dm, pooled, slope, p, w.reshape(towers, 9 * cin, cout), mix)


def swap(block):
    return lax.ppermute(block, "tower", [(0, 1), (1, 0)])


def shards(crop_pixels, live_rows, conv_weight, conv_bias, stitch_conv, fc_weight, fc_bias, stitch_fc, cotangent):
    slots = crop_pixels.shape[0]
    nb = lax.axis_size("batch")
    b, t = lax.axis_index("batch"), lax.axis_index("tower")
    rows = 2 * slots * nb
    live = rows // 2
    fc = fc_weight.shape[2]
    per = fc_weight.shape[1]
    cols = fc // nb
    w = fc_weight[0]
    feat, pooled, slope, padded = conv_fwd(crop_pixels, conv_weight, conv_bias, stitch_conv, nb)
    both = ("batch", "tower")
    counts = lax.all_gather(live_rows, both, axis=0, tiled=True)
    got = lax.all_to_all(feat.transpose(1, 0, 2, 3).reshape(2 * nb, slots, per), both, 0, 0).reshape(rows, per)
    slot = jnp.arange(rows, dtype=jnp.int32)
    start = jnp.cumsum(counts) - counts
    place = jnp.where(slot % slots < counts[slot // slots], start[slot // slots] + slot % slots, -1)
    spread = (place[:, None] == jnp.arange(live, dtype=jnp.int32)[None]).astype(BF16)
    compact = lambda x: lax.dot_general(spread, x, (((0,), (0,)), ((), ())), preferred_element_type=F32).astype(BF16)
    expand = lambda x: jnp.dot(spread, x, preferred_element_type=F32).astype(BF16)
    f = compact(got)
    part = jnp.dot(f, w, preferred_element_type=F32)
    hidden = lax.psum_scatter(part, "batch", scatter_dimension=1, tiled=True)
    hidden = hidden + lax.dynamic_slice_in_dim(fc_bias[0], b * cols, cols)[None]
    value, slope_fc = gelu_pair(hidden)
    gate = value.astype(BF16)
    cot = compact(lax.all_to_all(cotangent[0].reshape(2 * slots, nb, cols).transpose(1, 0, 2), "batch", 0, 0).reshape(rows, cols))
    gate_other, cot_other = swap(gate).astype(F32), swap(cot).astype(F32)
    gate_own, cot_own = gate.astype(F32), cot.astype(F32)
    mix = lax.dynamic_slice_in_dim(stitch_fc, b * cols, cols, axis=2)
    own = jnp.where(t == 0, mix[0, 0], mix[1, 1])
    cross = jnp.where(t == 0, mix[0, 1], mix[1, 0])
    back = jnp.where(t == 0, mix[1, 0], mix[0, 1])
    stitched = (own[None] * gate_own + cross[None] * gate_other).astype(BF16)
    stitched = lax.all_to_all(expand(stitched).reshape(nb, 2 * slots, cols), "batch", 0, 0)
    stitched = stitched.transpose(1, 0, 2).reshape(1, 2 * slots, fc)
    d_own = jnp.sum(cot_own * gate_own, axis=0)
    d_cross = jnp.sum(cot_own * gate_other, axis=0)
    dh = ((own[None] * cot_own + back[None] * cot_other) * slope_fc).astype(BF16)
    sums = jnp.stack([d_own, d_cross, jnp.sum(dh.astype(F32), axis=0)])
    sums = lax.all_gather(sums, both, axis=0).reshape(nb, 2, 3, cols).transpose(1, 2, 0, 3).reshape(2, 3, fc)
    d_stitch_fc = jnp.stack([sums[0, :2], sums[1, 1::-1]])
    d_fc_bias = sums[:, 2]
    dh = lax.all_gather(dh, "batch", axis=1, tiled=True)
    d_fc_weight = lax.dot_general(f, dh, (((0,), (0,)), ((), ())), preferred_element_type=F32)[None]
    df = lax.dot_general(dh, w, (((1,), (1,)), ((), ())), preferred_element_type=F32).astype(BF16)
    dm = lax.all_to_all(expand(df).reshape(2 * nb, slots, per), both, 0, 0)
    dm = dm.reshape(nb, 2, slots, per).transpose(1, 0, 2, 3)
    dx, dw, small = conv_bwd(dm, pooled, slope, padded, conv_weight, stitch_conv)
    dw = lax.psum(dw, both)
    cin, cout = conv_weight.shape[3:]
    dw = dw.reshape(3, 2, cout, 3, cin).transpose(1, 0, 3, 4, 2)
    small = lax.psum(small, both)
    d_conv_bias = small[:, 0].reshape(2, cout)
    d_stitch_conv = small[:, 128:130].T.reshape(2, 2, cout)
    return stitched, dx, dw, d_conv_bias, d_stitch_conv, d_fc_weight, d_fc_bias, d_stitch_fc


def solution(mesh):
    in_specs = (
        P(("batch", "tower"), None, None, None), P(("batch", "tower")), P(), P(), P(),
        P("tower", "batch", None), P("tower", None), P(), P("tower", "batch", None),
    )
    out_specs = (
        P("tower", "batch", None), P(("batch", "tower"), None, None, None), P(), P(), P(),
        P("tower", "batch", None), P(), P(),
    )
    return jax.shard_map(shards, mesh=mesh, in_specs=in_specs, out_specs=out_specs, check_vma=False)
```

time: 3210 us -> 581 us (0.18)
  waiting for transfers between devices: 2640 us -> 265 us
  matrix products: 207 us -> 18.1 us
  local copies, waits for them, and re-layouts: 199 us -> 43.5 us
  blocking collectives: 39.8 us -> 108 us
  Pallas kernels: 0 us -> 65.5 us
  other arithmetic: 86.8 us -> 43.3 us
    reduce_scatter x1, waiting for transfers between devices: 2060 us -> 73.7 us  [shards(): hidden = lax.psum_scatter(part, 'batch', scatter_dimension=1, tiled=True)]
    all_gather x1, waiting for transfers between devices: 577 us -> 65.4 us  [shards(): dh = lax.all_gather(dh, 'batch', axis=1, tiled=True)]
    dot_general x30 -> x6, matrix products: 207 us -> 18.1 us  [the longest x1 6.18 us: shards(): part = jnp.dot(f, w, preferred_element_type=F32)]
    psum x1, waiting for transfers between devices: 0.01 us -> 112 us  [shards(): dw = lax.psum(dw, both)]
    slice x24 -> x3, local copies, waits for them, and re-layouts: 76.7 us -> 2.12 us  [the longest x1 1.09 us: shards(): d_conv_bias = small[:, 0].reshape(2, cout)]
    reshape x22 -> x4, local copies, waits for them, and re-layouts: 85.1 us -> 11.2 us  [the longest x1 9.4 us: shards(): dw = dw.reshape(3, 2, cout, 3, cin).transpose(1, 0, 3, 4, 2)]
    scatter-add x9 -> x0, other arithmetic: 66.2 us -> none  [shards(): d_activated = d_activated.at[:, row_tap:row_tap + span:2, col_tap:col_tap...]
    pallas_call x0 -> x2, Pallas kernels: none -> 65.5 us  [the longest x1 42.2 us: conv_bwd(): pl.pallas_call(conv_bwd_kernel, out_shape=[jax.ShapeDtypeStruct((slots, s...]
  transfers between devices with their start and end apart: 8 -> 8, of which waited for: 3 -> 6; matrix products, arithmetic and copies ran while one was open for 13% -> 10% of each run, Pallas kernels for 0% -> 0%
where the time goes in v1:
time: 581 us; the launch traced here: 578 us
  waiting for transfers between devices  265 us (46%)
  blocking collectives  108 us (19%)
  Pallas kernels  65.5 us (11%)
  local copies, waits for them, and re-layouts  43.5 us (7%)
  other arithmetic  43.3 us (7%)
  starting transfers between devices  20.7 us (4%)
  matrix products  18.1 us (3%)
  between operations  14.6 us (3%)
    psum x1, waiting for transfers between devices, shards(): dw = lax.psum(dw, both)  112 us
    reduce_scatter x1, waiting for transfers between devices, shards(): hidden = lax.psum_scatter(part, 'batch', scatter_dimension=1, tiled=True)  73.7 us
    all_gather x1, waiting for transfers between devices, shards(): dh = lax.all_gather(dh, 'batch', axis=1, tiled=True)  65.4 us
    all_gather x1, blocking collectives, shards(): lax.all_gather(sums, both, axis=0).reshape(nb, 2, 3, cols)  46 us
    pallas_call x1, Pallas kernels, conv_bwd(): pl.pallas_call(conv_bwd_kernel, out_shape=[jax.ShapeDtypeStruct((slots, s...  42.2 us
    unnamed x1, blocking collectives  39.6 us
    select_n x1, other arithmetic, shards(): jnp.where(slot % slots < counts[slot // slots], start[slot // slots] + sl...  31 us
    pallas_call x1, Pallas kernels, conv_fwd(): pl.pallas_call(functools.partial(conv_fwd_kernel, rows_per), out_shape=[j...  23.3 us
  transfers between devices with their start and end apart: 8, of which 6 were waited for; matrix products, arithmetic and copies ran while one was open for 10% of the time, Pallas kernels for 0%

profile of v1, /device:TPU:1, one launch (start us, length us, event | category | flops | bytes accessed | tf_op | source)
XLA Modules:
  0.0 578.4 jit_solution(17079317033587500180)
XLA Ops:
  7.2 3.6 copy.47.x_ref
  10.8 23.3 %shard_map.152 = (bf16[2,16,16,576]{3,2,1,0:T(8,128)(2,1)}, f32[36,16,512]{2,1,0:T(8,128)}, bf16[13,13,16,512]{3,2,1,0:T(8,128)(2,1)}, bf16[15,15,16,384]{3,2,1,0:T(8,128)(2,1)}) custom-call(bf16[16,13,13,384]{3,2,1,0:T(8,128)(2,1)} %copy.47.x_ref, bf16[2,3456,256]{2,1,0:T(8,128)(2,1)} %bitcast.123, f32[2,256]{1,0:T(2,128)} %b_ref.1, f32[2,2,256]{2,1,0:T(2,128)} %mix_ref.3), custom_call_target="tpu_custom_call" | custom-call | tf_op jit(solution)/shard_map/pallas_call | solution.py:72
  34.1 2.0 copy.48
  36.1 7.1 %all-to-all-start = ((bf16[32,16,576]{2,1,0:T(8,128)(2,1)}), bf16[32,16,576]{2,1,0:T(8,128)(2,1)S(1)}, u32[]{:S(2)}, u32[]{:S(2)}) async-start(bf16[32,16,576]{2,1,0:T(8,128)(2,1)} %bitcast.70), calls=%async_computation | async-start | bytes 1310720 | tf_op jit(solution)/shard_map/all_to_all | solution.py:203
  44.0 39.6 %all-reduce = s32[32]{0:T(128)S(1)} all-reduce(s32[32]{0:T(128)S(1)} %dynamic-update-slice), channel_id=1, replica_groups=mesh['batch'=16,'tower'=2] {'batch','tower'}, use_global_device_ids=true, to_apply=%add | all-reduce | flops 32 | bytes 256
  84.7 0.7 fusion.34
  85.4 4.3 compare_select_fusion.2
  89.7 0.7 fusion.32
  90.4 4.2 compare_select_fusion.1
  94.6 0.7 fusion.33
  95.4 0.7 fusion.31
  96.1 31.0 %fusion.25 = s32[512]{0:T(512)S(1)} fusion(pred[512]{0:T(512)(128)(4,1)S(1)} %compare_reduce_fusion, pred[512]{0:T(512)(128)(4,1)S(1)} %compare_reduce_fusion.1, pred[512]{0:T(512)(128)(4,1)S(1)} %compare_reduce_fusion.2, pred[512]{0:T(512)(128)(4,1)S(1)} %compare_reduce_fusion.3, pred[512]{0:T(512)(128)(4,1)S(1)} %compare_reduce_fusion.4, ...), kind=kLoop, calls=%fused_computation.82 | loop fusion | flops 30208 | bytes 19144 | tf_op jit(solution)/shard_map/jit(_where)/select_n | solution.py:206
  127.1 0.5 convolution_convert_fusion.1
  127.6 6.2 %fusion.2 = f32[256,4096]{1,0:T(8,128)} fusion(bf16[256,576]{0,1:T(8,128)(2,1)S(1)} %convolution_convert_fusion.1, bf16[1,576,4096]{2,1,0:T(8,128)(2,1)} %param.14), kind=kOutput, calls=%fused_computation.3 | convolution fusion | flops 1207959552 | bytes 9207808 | tf_op jit(solution)/shard_map/dot_general | solution.py:211
  133.8 0.9 copy-done.4
  134.8 0.8 copy.50
  135.6 5.3 all-to-all-start.2
  140.9 12.7 %all-to-all-done.2 = bf16[16,32,256]{2,1,0:T(8,128)(2,1)S(1)} async-done(((bf16[16,32,256]{2,1,0:T(8,128)(2,1)}), bf16[16,32,256]{2,1,0:T(8,128)(2,1)S(1)}, u32[]{:S(2)}, u32[]{:S(2)}) %all-to-all-start.2) | async-done | bytes 262176 | tf_op jit(solution)/shard_map/all_to_all | solution.py:216
  153.6 0.4 convolution_convert_fusion.3
  154.0 3.5 collective-permute-start.1
  157.5 0.8 broadcast_select_fusion
  158.5 73.7 %reduce-scatter.2.cloned.1.call-done = f32[256,256]{1,0:T(8,128)} async-done(((f32[256,4096]{1,0:T(8,128)}), f32[256,256]{1,0:T(8,128)}) %reduce-scatter.2.cloned.1.call-update) | async-done | bytes 262160 | tf_op jit(solution)/shard_map/reduce_scatter | solution.py:212
  232.2 1.8 convert_reduce_fusion
  234.0 65.4 %all-gather.4.cloned.1.call-done = bf16[256,4096]{1,0:T(8,128)(2,1)} async-done(((bf16[256,256]{1,0:T(8,128)(2,1)}), bf16[256,4096]{1,0:T(8,128)(2,1)}) %all-gather.4.cloned.1.call-update) | async-done | bytes 2097168 | tf_op jit(solution)/shard_map/all_gather | solution.py:233
  299.5 4.8 convolution_convert_fusion
  304.3 0.3 copy.51
  304.6 22.2 %all_to_all.20 = bf16[32,16,576]{2,1,0:T(8,128)(2,1)S(1)} all-to-all(bf16[32,16,576]{2,1,0:T(8,128)(2,1)S(1)} %bitcast.125), channel_id=1, replica_groups=mesh['batch'=16,'tower'=2] {'batch','tower'}, dimensions={0} | all-to-all | bytes 1179648 | tf_op jit(solution)/shard_map/all_to_all | solution.py:236
  326.8 0.9 copy.62
  327.7 42.2 %shard_map.153 = (bf16[16,13,13,384]{3,2,1,0:T(8,128)(2,1)}, f32[3,512,1152]{2,1,0:T(8,128)}, f32[512,256]{1,0:T(8,128)}) custom-call(bf16[2,16,16,576]{3,2,1,0:T(8,128)(2,1)} %bitcast.127, f32[36,16,512]{2,1,0:T(8,128)} %get-tuple-element.16.pooled_ref, bf16[13,13,16,512]{3,2,1,0:T(8,128)(2,1)} %get-tuple-element.17.slope_ref, ...), custom_call_target="tpu_custom_call" | custom-call | tf_op jit(solution)/shard_map/pallas_call | solution.py:170
  369.9 8.0 %copy.53 = f32[3,512,1152]{1,2,0:T(8,128)} copy(f32[3,512,1152]{2,1,0:T(8,128)} %get-tuple-element.20) | data formatting | bytes 14155776 | tf_op jit(solution)/shard_map/pallas_call | solution.py:170
  377.9 9.4 %reshape.183 = f32[3,2,256,3,384]{2,1,4,3,0:T(2,128)} reshape(f32[3,512,1152]{1,2,0:T(8,128)} %copy.53) | data formatting | bytes 14155776 | tf_op jit(solution)/shard_map/reshape | solution.py:241
  387.4 0.5 collective-permute-start
  387.9 1.0 collective-permute-done
  388.9 1.0 convolution_convert_fusion.2
  389.9 4.2 all-to-all-start.1
  394.2 46.0 %all-gather.1 = f32[32,3,256]{2,1,0:T(4,128)S(1)} all-gather(f32[1,3,256]{2,1,0:T(4,128)S(1)} %maximum_bitcast_fusion), channel_id=2, replica_groups=mesh['batch'=16,'tower'=2] {'batch','tower'}, dimensions={0}, use_global_device_ids=true | all-gather | bytes 101376 | tf_op jit(solution)/shard_map/all_gather | solution.py:230
  440.4 0.7 copy.58
  441.0 0.6 slice_bitcast_fusion
  441.7 0.1 copy.49
  441.8 0.8 reshape.179
  442.6 5.1 convolution_bitcast_fusion
  447.8 1.8 copy.55
  449.6 112.0 %all-reduce.4.cloned.1.call-done = (f32[2,3,3,384,256]{4,0,3,2,1:T(2,128)}, f32[512,256]{1,0:T(8,128)}) async-done(((f32[2,3,3,384,256]{4,0,3,2,1:T(2,128)}, f32[512,256]{1,0:T(8,128)}), (f32[2,3,3,384,256]{4,0,3,2,1:T(2,128)}, f32[512,256]{1,0:T(8,128)})) %all-reduce.4.cloned.1.call-update) | async-done | bytes 7602192 | tf_op jit(solution)/shard_map/psum | solution.py:239
  561.6 1.1 slice_reduce_fusion
  562.7 1.0 slice.105
  563.7 6.8 %copy.56 = f32[2,3,3,384,256]{4,3,2,1,0:T(8,128)} copy(f32[2,3,3,384,256]{4,0,3,2,1:T(2,128)} %get-tuple-element.56) | data formatting | bytes 14155776
  570.5 0.6 reshape_squeeze.7
  571.1 0.7 copy.57
  (57 shorter events, 1.9 us)
Async XLA Ops:
  7.2 150.4 %copy-start = (f32[1,4096]{1,0:T(1,128)S(1)}, f32[1,4096]{1,0:T(1,128)}, u32[]{:S(2)}) copy-start(f32[1,4096]{1,0:T(1,128)} %param.15) | copy-start | bytes 49156
  36.1 91.1 %all-to-all-start = ((bf16[32,16,576]{2,1,0:T(8,128)(2,1)}), bf16[32,16,576]{2,1,0:T(8,128)(2,1)S(1)}, u32[]{:S(2)}, u32[]{:S(2)}) async-start(bf16[32,16,576]{2,1,0:T(8,128)(2,1)} %bitcast.70), calls=%async_computation | async-start | bytes 1310720 | tf_op jit(solution)/shard_map/all_to_all | solution.py:203
  43.2 189.0 %reduce-scatter.2.cloned.1.call-start = ((), (), s32[]{:S(2)}) async-start(), calls=%async_computation.5 | async-start | bytes 4456448 | tf_op jit(solution)/shard_map/reduce_scatter | solution.py:212
  133.8 0.9 copy-start.4
  135.6 18.0 %all-to-all-start.2 = ((bf16[16,32,256]{2,1,0:T(8,128)(2,1)}), bf16[16,32,256]{2,1,0:T(8,128)(2,1)S(1)}, u32[]{:S(2)}, u32[]{:S(2)}) async-start(bf16[16,32,256]{2,1,0:T(8,128)(2,1)} %copy.50), calls=%async_computation.3 | async-start | bytes 524288 | tf_op jit(solution)/shard_map/all_to_all | solution.py:216
  140.8 158.6 %all-gather.4.cloned.1.call-start = ((), (), s32[]{:S(2)}) async-start(), calls=%async_computation.6 | async-start | bytes 2228224 | tf_op jit(solution)/shard_map/all_gather | solution.py:233
  154.0 4.5 collective-permute-start.1
  234.0 327.6 %all-reduce.4.cloned.1.call-start = ((), (), s32[]{:S(2)}) async-start(), calls=%async_computation.7 | async-start | bytes 15204352 | tf_op jit(solution)/shard_map/psum | solution.py:239
  387.3 55.3 %copy-start.3 = (bf16[256,4096]{1,0:T(8,128)(2,1)S(1)}, bf16[256,4096]{1,0:T(8,128)(2,1)}, u32[]{:S(2)}) copy-start(bf16[256,4096]{1,0:T(8,128)(2,1)} %all-gather.4.cloned.1.call-done) | copy-start | bytes 6291460
  387.4 1.5 collective-permute-start
  389.9 51.8 %all-to-all-start.1 = ((bf16[16,32,256]{2,1,0:T(8,128)(2,1)}), bf16[16,32,256]{2,1,0:T(8,128)(2,1)S(1)}, u32[]{:S(2)}, u32[]{:S(2)}) async-start(bf16[16,32,256]{2,1,0:T(8,128)(2,1)} %bitcast.75), calls=%async_computation.2 | async-start | bytes 524288 | tf_op jit(solution)/shard_map/all_to_all | solution.py:224
  442.6 5.1 copy-start.2
  563.7 8.2 %copy-start.1 = (f32[1,4096]{1,0:T(1,128)S(1)}, f32[1,4096]{1,0:T(1,128)}, u32[]{:S(2)}) copy-start(f32[1,4096]{1,0:T(1,128)} %param.15) | copy-start | bytes 49156
Sparse Core Ops, SparseCore 0:
  133.9 98.1 reduce-scatter.1
  235.5 63.9 all-gather.3
  387.5 174.0 all-reduce.3

commit v2 on v1

--- a/solution.py
+++ b/solution.py
@@ -15,7 +15,7 @@
     slope = half + value * (1.0 - half) * (2.0 * CG + (6.0 * CG * 0.044715) * sq)
     return value, slope
 
-def conv_fwd_kernel(rows_per, x_ref, w_ref, b_ref, mix_ref, feat_ref, pooled_ref, slope_ref, p_ref, stage, act, fbuf):
+def conv_fwd_kernel(rows_per, live_ref, x_ref, w_ref, b_ref, mix_ref, feat_ref, pooled_ref, slope_ref, p_ref, stage, act, fbuf):
     slots, side, _, cin = x_ref.shape
     towers, _, cout = w_ref.shape
     pool = (side - 3) // 2 + 1
@@ -58,12 +58,15 @@
             for t in range(towers):
                 m = mix_ref[t, 0][None] * p9[:, :cout] + mix_ref[t, 1][None] * p9[:, cout:]
                 fbuf[t, :, (i * pool + j) * cout:(i * pool + j + 1) * cout] = m.astype(BF16)
-    nb, per = feat_ref.shape[1], feat_ref.shape[3]
+    nb = feat_ref.shape[1]
+    per = fbuf.shape[2] // nb
+    flags = (lax.broadcasted_iota(jnp.int32, (slots, feat_ref.shape[3] - per), 0) < live_ref[0]).astype(F32).astype(BF16)
     for t in range(towers):
         for b in range(nb):
-            feat_ref[t, b] = fbuf[t, :, b * per:(b + 1) * per]
-
-def conv_fwd(x, w, bias, mix, nb, rows_per=1):
+            feat_ref[t, b, :, :per] = fbuf[t, :, b * per:(b + 1) * per]
+            feat_ref[t, b, :, per:] = flags
+
+def conv_fwd(live, x, w, bias, mix, nb, rows_per=1):
     slots, side, _, cin = x.shape
     towers, _, _, _, cout = w.shape
     pool = (side - 3) // 2 + 1
@@ -71,20 +74,325 @@
     V = pl.BlockSpec(memory_space=pltpu.VMEM)
     return pl.pallas_call(
         functools.partial(conv_fwd_kernel, rows_per),
-        out_shape=[jax.ShapeDtypeStruct((towers, nb, slots, nf // nb), BF16),
+        out_shape=[jax.ShapeDtypeStruct((towers, nb, slots, nf // nb // 128 * 128 + 128), BF16),
                    jax.ShapeDtypeStruct((pool * pool, slots, towers * cout), F32),
                    jax.ShapeDtypeStruct((side, side, slots, towers * cout), BF16),
                    jax.ShapeDtypeStruct((side + 2, side + 2, slots, cin), BF16)],
-        in_specs=[V] * 4, out_specs=[V] * 4,
+        in_specs=[pl.BlockSpec(memory_space=pltpu.SMEM)] + [V] * 4, out_specs=[V] * 4,
         scratch_shapes=[pltpu.VMEM((cin // 128, slots * side * 16, 128), F32),
                         pltpu.VMEM((side, side, slots, towers * cout), F32),
                         pltpu.VMEM((towers, slots, nf), BF16)],
         compiler_params=pltpu.CompilerParams(vmem_limit_bytes=60 * 2**20),
-    )(x, w.reshape(towers, 9 * cin, cout), bias, mix)
+    )(live, x, w.reshape(towers, 9 * cin, cout), bias, mix)
+
+
+MESH_ID = pl.DeviceIdType.MESH
+
+
+def torus(nb):
+    return {16: (4, 2, 2), 64: (4, 4, 4)}.get(nb, (nb, 1, 1))
+
+
+class Place:
+    def __init__(self, nb):
+        self.dims = torus(nb)
+        self.b, self.t = lax.axis_index("batch"), lax.axis_index("tower")
+        d0, d1, d2 = self.dims
+        self.at = (self.b // (d1 * d2), (self.b // d2) % d1, self.b % d2)
+
+    def peer(self, dim, k):
+        c = list(self.at)
+        c[dim] = k
+        return ((c[0] * self.dims[1] + c[1]) * self.dims[2] + c[2], self.t)
+
+
+def send(src, dst, ssem, rsem, device):
+    copy = pltpu.make_async_remote_copy(src_ref=src, dst_ref=dst, send_sem=ssem, recv_sem=rsem, device_id=device, device_id_type=MESH_ID)
+    copy.start()
+    return copy
+
+
+def greet(nb, me):
+    bar = pltpu.get_barrier_semaphore()
+    total = 2 * nb
+    def hail(k, _):
+        d = lax.rem(me + k, total)
+        pl.semaphore_signal(bar, inc=1, device_id=(d // 2, d % 2), device_id_type=MESH_ID)
+        return 0
+    lax.fori_loop(1, total, hail, 0)
+    pl.semaphore_wait(bar, total - 1)
+
+
+class Sum:
+    def __init__(self, place, p, s, r1, t1, r2, t2, r3, g, ssem, rsem):
+        self.place, self.p, self.q = place, p, 3 - p
+        self.s, self.r1, self.t1, self.r2, self.t2, self.r3, self.g = s, r1, t1, r2, t2, r3, g
+        self.ssem, self.rsem = ssem, rsem
+        self.sent = []
+        self.used = 0
+
+    def pick(self, ref, k):
+        return ref.at[:, :, k] if self.p == 2 else ref.at[:, k]
+
+    def post(self, dim, src_of, dst_of):
+        n = self.place.dims[dim]
+        self.flight = []
+        for j in range(1, n):
+            k = lax.rem(self.place.at[dim] + j, n)
+            i = self.used
+            self.used += 1
+            self.flight.append(send(src_of(k), dst_of(j - 1), self.ssem.at[i], self.rsem.at[i], self.place.peer(dim, k)))
+        self.sent += self.flight
+
+    def arrive(self):
+        for c in self.flight:
+            c.wait_recv()
+
+    def add(self, mine, got, n):
+        v = mine.astype(F32)
+        for j in range(n):
+            v = v + got[j].astype(F32)
+        return v
+
+    def send1(self):
+        self.post(self.p, lambda k: self.pick(self.s, k), lambda j: self.r1.at[j])
+
+    def send2(self):
+        self.arrive()
+        n = self.place.dims[self.p]
+        self.t1[...] = self.add(self.pick(self.s, self.place.at[self.p])[...], self.r1, n - 1).astype(BF16)
+        self.post(self.q, lambda k: self.t1.at[:, k], lambda j: self.r2.at[j])
+
+    def send3(self):
+        self.arrive()
+        n = self.place.dims[self.q]
+        self.t2[...] = self.add(self.t1[:, self.place.at[self.q]], self.r2, n - 1).astype(BF16)
+        self.post(0, lambda k: self.t2.at[k], lambda j: self.r3.at[j])
+
+    def result(self):
+        self.arrive()
+        return self.add(self.t2[self.place.at[0]], self.r3, self.place.dims[0] - 1)
+
+    def gather1(self):
+        mine = self.g.at[self.place.at[0], self.place.at[1], self.place.at[2]]
+        self.post(0, lambda k: mine, lambda j: mine)
+
+    def gather2(self):
+        self.arrive()
+        mine = self.g.at[:, self.place.at[1], self.place.at[2]]
+        self.post(self.q, lambda k: mine, lambda j: mine)
+
+    def gather3(self):
+        self.arrive()
+        mine = self.pick(self.g, self.place.at[self.p])
+        self.post(self.p, lambda k: mine, lambda j: mine)
+
+    def close(self):
+        for c in self.sent:
+            c.wait_send()
+
+
+def hops(nb):
+    return 2 * sum(d - 1 for d in torus(nb))
+
+
+def fc_kernel(parts, nb, per, feat_ref, cot_ref, w_hbm, bias_ref, mix_ref,
+              out_ref, f_ref, dh_ref, dm_ref, sums_ref,
+              w, fin, cin, cgot, spread, s, r1, t1, r2, t2, r3, g, keep, gates, cots, wide, st, sgot, dsl, acc,
+              wsem, fs, fr, cs, cr, xs, xr, ss, sr, ms, mr, gs, gr):
+    place = Place(nb)
+    b, t = place.b, place.t
+    me = b * 2 + t
+    total = 2 * nb
+    slots = feat_ref.shape[2]
+    rows = total * slots
+    live = rows // 2
+    cols = cin.shape[2]
+    pair = 2 * slots
+    load = pltpu.make_async_copy(w_hbm, w, wsem)
+    load.start()
+    greet(nb, me)
+    def feature_copy(k):
+        d = lax.rem(me + k, total)
+        return pltpu.make_async_remote_copy(
+            src_ref=feat_ref.at[d % 2, d // 2], dst_ref=fin.at[me], send_sem=fs.at[k], recv_sem=fr.at[k],
+            device_id=(d // 2, d % 2), device_id_type=MESH_ID)
+    lax.fori_loop(1, total, lambda k, _: (feature_copy(k).start(), 0)[1], 0)
+    fin[me] = feat_ref[t, b]
+    for k in range(nb):
+        cin[k] = cot_ref[:, k * cols:(k + 1) * cols]
+    def cot_copy(k):
+        d = lax.rem(b + k, nb)
+        return pltpu.make_async_remote_copy(
+            src_ref=cin.at[d], dst_ref=cgot.at[b], send_sem=cs.at[k], recv_sem=cr.at[k],
+            device_id=(d, t), device_id_type=MESH_ID)
+    lax.fori_loop(1, nb, lambda k, _: (cot_copy(k).start(), 0)[1], 0)
+    cgot[b] = cin[b]
+    lax.fori_loop(1, total, lambda k, _: (feature_copy(k).wait_recv(), 0)[1], 0)
+    got = fin[...].reshape(rows, fin.shape[2])
+    flag = got[:, per:per + 1]
+    lanes = jnp.broadcast_to(flag, (rows, 128))
+    lower = (lax.broadcasted_iota(jnp.int32, (rows, rows), 1) < lax.broadcasted_iota(jnp.int32, (rows, rows), 0)).astype(BF16)
+    index = jnp.dot(lower, lanes, preferred_element_type=F32)[:, :1].astype(jnp.int32)
+    hit = (index == lax.broadcasted_iota(jnp.int32, (rows, live), 1)) & (flag.astype(F32) > 0.5)
+    spread[...] = hit.astype(F32).astype(BF16)
+    pack = lambda x: lax.dot_general(spread[...], x, (((0,), (0,)), ((), ())), preferred_element_type=F32)
+    f_ref[...] = pack(got[:, :per]).astype(BF16)
+    load.wait()
+    for k in range(nb):
+        i = (k // (place.dims[1] * place.dims[2]), (k // place.dims[2]) % place.dims[1], k % place.dims[2])
+        s[i] = jnp.dot(f_ref[...], w[:, k * cols:(k + 1) * cols], preferred_element_type=F32).astype(BF16)
+    size = live // (2 * parts)
+    pieces = []
+    for n in range(2 * parts):
+        half = n % 2
+        low = pl.ds(((n // 2) + half * parts) * size, size)
+        pieces.append((Sum(place, 2 - half, s.at[:, :, :, low], r1.at[n], t1.at[n], r2.at[n], t2.at[n], r3.at[n],
+                           g.at[:, :, :, low], gs.at[n], gr.at[n]), low))
+    for piece, _ in pieces:
+        piece.send1()
+    lax.fori_loop(1, nb, lambda k, _: (cot_copy(k).wait_recv(), 0)[1], 0)
+    cots[0] = pack(cgot[...].reshape(rows, cols)).astype(BF16)
+    other = (b, 1 - t)
+    cot_swap = send(cots.at[0], cots.at[1], xs.at[0], xr.at[0], other)
+    stages = [lambda p, low: p.send2(), lambda p, low: p.send3()]
+    def mixes(i, j):
+        return mix_ref[i, j]
+    first = t == 0
+    own = jnp.where(first, mixes(0, 0), mixes(1, 1))
+    cross = jnp.where(first, mixes(0, 1), mixes(1, 0))
+    back = jnp.where(first, mixes(1, 0), mixes(0, 1))
+    def finish(piece, low):
+        value, slope = gelu_pair(piece.result() + bias_ref[...])
+        gates[0, low, :] = value.astype(BF16)
+        d_gate = own * cots[0, low, :].astype(F32) + back * cots[1, low, :].astype(F32)
+        g[place.at[0], place.at[1], place.at[2], low, :] = (d_gate * slope).astype(BF16)
+        piece.gather1()
+    def phase3(piece, low):
+        piece.gather2()
+    def phase4(piece, low):
+        piece.gather3()
+    swapped = False
+    todo = [lambda p, low: p.send2(), lambda p, low: p.send3(), finish]
+    steps = len(pieces) // 2
+    for step in range(steps + 2):
+        for k in range(3):
+            c = step - k
+            if 0 <= c < steps:
+                if k == 2 and not swapped:
+                    cot_swap.wait_recv()
+                    swapped = True
+                for piece, low in pieces[2 * c:2 * c + 2]:
+                    todo[k](piece, low)
+    gate_swap = send(gates.at[0], gates.at[1], xs.at[1], xr.at[1], other)
+    for piece, low in pieces[:2]:
+        piece.gather2()
+    gate_swap.wait_recv()
+    gate, cot, gate_other = gates[0].astype(F32), cots[0].astype(F32), gates[1].astype(F32)
+    mine = g.at[place.at[0], place.at[1], place.at[2]]
+    zero = jnp.zeros((1, cols), F32)
+    total_rows = [jnp.sum(cot * gate, axis=0, keepdims=True), jnp.sum(cot * gate_other, axis=0, keepdims=True),
+                  jnp.sum(mine[...].astype(F32), axis=0, keepdims=True)]
+    wide[me] = jnp.concatenate(total_rows + [zero] * 5, axis=0)
+    def sums_copy(k):
+        d = lax.rem(me + k, total)
+        return pltpu.make_async_remote_copy(
+            src_ref=wide.at[me], dst_ref=wide.at[me], send_sem=ms.at[k], recv_sem=mr.at[k],
+            device_id=(d // 2, d % 2), device_id_type=MESH_ID)
+    stitched = (own * gate + cross * gate_other).astype(BF16)
+    st[...] = jnp.dot(spread[...], stitched, preferred_element_type=F32).astype(BF16).reshape(st.shape)
+    def stitched_copy(k):
+        d = lax.rem(b + k, nb)
+        return pltpu.make_async_remote_copy(
+            src_ref=st.at[d], dst_ref=sgot.at[b], send_sem=ss.at[k], recv_sem=sr.at[k],
+            device_id=(d, t), device_id_type=MESH_ID)
+    lax.fori_loop(1, total, lambda k, _: (sums_copy(k).start(), 0)[1], 0)
+    lax.fori_loop(1, nb, lambda k, _: (stitched_copy(k).start(), 0)[1], 0)
+    sgot[b] = st[b]
+    for c in range(1, steps):
+        for piece, low in pieces[2 * c:2 * c + 2]:
+            piece.gather2()
+        for piece, low in pieces[2 * c - 2:2 * c]:
+            piece.gather3()
+    for piece, low in pieces[-2:]:
+        piece.gather3()
+    for piece, low in pieces:
+        piece.arrive()
+    acc[...] = jnp.zeros(acc.shape, F32)
+    for k in range(nb):
+        i = (k // (place.dims[1] * place.dims[2]), (k // place.dims[2]) % place.dims[1], k % place.dims[2])
+        acc[...] += lax.dot_general(g[i], w[:, k * cols:(k + 1) * cols], (((1,), (1,)), ((), ())), preferred_element_type=F32)
+    df = jnp.dot(spread[...], acc[...].astype(BF16), preferred_element_type=F32).astype(BF16)
+    dsl[:, :, :per] = df.reshape(total, slots, per)
+    def grad_copy(k):
+        d = lax.rem(me + k, total)
+        return pltpu.make_async_remote_copy(
+            src_ref=dsl.at[d], dst_ref=dm_ref.at[t, b], send_sem=fs.at[k + total], recv_sem=fr.at[k + total],
+            device_id=(d // 2, d % 2), device_id_type=MESH_ID)
+    lax.fori_loop(1, total, lambda k, _: (grad_copy(k).start(), 0)[1], 0)
+    dm_ref[t, b] = dsl[me]
+    for k in range(nb):
+        i = (k // (place.dims[1] * place.dims[2]), (k // place.dims[2]) % place.dims[1], k % place.dims[2])
+        dh_ref[:, k * cols:(k + 1) * cols] = g[i]
+    lax.fori_loop(1, nb, lambda k, _: (stitched_copy(k).wait_recv(), 0)[1], 0)
+    for k in range(nb):
+        out_ref[0, :, k * cols:(k + 1) * cols] = sgot[k]
+    lax.fori_loop(1, total, lambda k, _: (sums_copy(k).wait_recv(), 0)[1], 0)
+    for k in range(nb):
+        for u in range(2):
+            sums_ref[u, :, k * cols:(k + 1) * cols] = wide[2 * k + u]
+    lax.fori_loop(1, total, lambda k, _: (grad_copy(k).wait_recv(), 0)[1], 0)
+    for piece, _ in pieces:
+        piece.close()
+    cot_swap.wait_send()
+    gate_swap.wait_send()
+    def drain(k, _):
+        feature_copy(k).wait_send()
+        grad_copy(k).wait_send()
+        sums_copy(k).wait_send()
+        return 0
+    lax.fori_loop(1, total, drain, 0)
+    def drain2(k, _):
+        cot_copy(k).wait_send()
+        stitched_copy(k).wait_send()
+        return 0
+    lax.fori_loop(1, nb, drain2, 0)
+
+
+def fc_layer(feat, cot, w, bias, mix, nb, per, parts=2):
+    _, _, slots, padded = feat.shape
+    fc = w.shape[1]
+    cols = fc // nb
+    total = 2 * nb
+    rows = total * slots
+    live = rows // 2
+    d0, d1, d2 = torus(nb)
+    size = live // (2 * parts)
+    V = pl.BlockSpec(memory_space=pltpu.VMEM)
+    vm = lambda *shape: pltpu.VMEM(shape, BF16)
+    dma = lambda *shape: pltpu.SemaphoreType.DMA(shape)
+    n = 2 * parts
+    return pl.pallas_call(
+        functools.partial(fc_kernel, parts, nb, per),
+        out_shape=[jax.ShapeDtypeStruct((1, 2 * slots, fc), BF16), jax.ShapeDtypeStruct((live, per), BF16),
+                   jax.ShapeDtypeStruct((live, fc), BF16), jax.ShapeDtypeStruct((2, nb, slots, padded), BF16),
+                   jax.ShapeDtypeStruct((2, 8, fc), F32)],
+        in_specs=[V, V, pl.BlockSpec(memory_space=pl.ANY), V, V], out_specs=[V] * 5,
+        scratch_shapes=[
+            vm(per, fc), vm(total, slots, padded), vm(nb, 2 * slots, cols), vm(nb, 2 * slots, cols), vm(rows, live),
+            vm(d0, d1, d2, live, cols), vm(n, d1 - 1, d0, d1, size, cols), vm(n, d0, d1, size, cols),
+            vm(n, d1 - 1, d0, size, cols), vm(n, d0, size, cols), vm(n, d0 - 1, size, cols), vm(d0, d1, d2, live, cols),
+            vm(16, 128), vm(2, live, cols), vm(2, live, cols), pltpu.VMEM((total, 8, cols), F32),
+            vm(nb, 2 * slots, cols), vm(nb, 2 * slots, cols), vm(total, slots, padded), pltpu.VMEM((live, per), F32),
+            pltpu.SemaphoreType.DMA, dma(2 * total), dma(2 * total), dma(nb), dma(nb), dma(2), dma(2), dma(nb), dma(nb),
+            dma(total), dma(total), dma(n, hops(nb)), dma(n, hops(nb))],
+        compiler_params=pltpu.CompilerParams(collective_id=1, has_side_effects=True, vmem_limit_bytes=60 * 2**20),
+    )(feat, cot, w, bias, mix)
 
 def conv_bwd_kernel(dm_ref, pooled_ref, slope_ref, p_ref, w_ref, mix_ref, dx_ref, dw_ref, small_ref,
                     fbuf, z, dpad, d2, dt, stage):
-    towers, nb, slots, per = dm_ref.shape
+    towers, nb, slots, _ = dm_ref.shape
+    per = fbuf.shape[2] // nb
     side = slope_ref.shape[0]
     cout = w_ref.shape[2]
     cin = p_ref.shape[3]
@@ -93,7 +401,7 @@
     cells = side * side
     for t in range(towers):
         for b in range(nb):
-            fbuf[t, :, b * per:(b + 1) * per] = dm_ref[t, b]
+            fbuf[t, :, b * per:(b + 1) * per] = dm_ref[t, b, :, :per]
     z[0] = jnp.zeros(z.shape[1:], F32)
     z[pool + 1] = jnp.zeros(z.shape[1:], F32)
     acc = [[jnp.zeros((slots, cout), F32)] * 2 for _ in range(2)]
@@ -158,8 +466,8 @@
         return 0
     lax.fori_loop(0, slots * side, put, 0, unroll=4)
 
-def conv_bwd(dm, pooled, slope, p, w, mix):
-    towers, nb, slots, per = dm.shape
+def conv_bwd(dm, pooled, slope, p, w, mix, per):
+    towers, nb, slots, _ = dm.shape
     side = slope.shape[0]
     cin = p.shape[3]
     cout = w.shape[4]
@@ -187,7 +495,7 @@
     return lax.ppermute(block, "tower", [(0, 1), (1, 0)])
 
 
-def shards(crop_pixels, live_rows, conv_weight, conv_bias, stitch_conv, fc_weight, fc_bias, stitch_fc, cotangent):
+def plain_shards(crop_pixels, live_rows, conv_weight, conv_bias, stitch_conv, fc_weight, fc_bias, stitch_fc, cotangent):
     slots = crop_pixels.shape[0]
     nb = lax.axis_size("batch")
     b, t = lax.axis_index("batch"), lax.axis_index("tower")
@@ -197,10 +505,10 @@
     per = fc_weight.shape[1]
     cols = fc // nb
     w = fc_weight[0]
-    feat, pooled, slope, padded = conv_fwd(crop_pixels, conv_weight, conv_bias, stitch_conv, nb)
+    feat, pooled, slope, padded = conv_fwd(live_rows, crop_pixels, conv_weight, conv_bias, stitch_conv, nb)
     both = ("batch", "tower")
     counts = lax.all_gather(live_rows, both, axis=0, tiled=True)
-    got = lax.all_to_all(feat.transpose(1, 0, 2, 3).reshape(2 * nb, slots, per), both, 0, 0).reshape(rows, per)
+    got = lax.all_to_all(feat[..., :per].transpose(1, 0, 2, 3).reshape(2 * nb, slots, per), both, 0, 0).reshape(rows, per)
     slot = jnp.arange(rows, dtype=jnp.int32)
     start = jnp.cumsum(counts) - counts
     place = jnp.where(slot % slots < counts[slot // slots], start[slot // slots] + slot % slots, -1)
@@ -235,7 +543,32 @@
     df = lax.dot_general(dh, w, (((1,), (1,)), ((), ())), preferred_element_type=F32).astype(BF16)
     dm = lax.all_to_all(expand(df).reshape(2 * nb, slots, per), both, 0, 0)
     dm = dm.reshape(nb, 2, slots, per).transpose(1, 0, 2, 3)
-    dx, dw, small = conv_bwd(dm, pooled, slope, padded, conv_weight, stitch_conv)
+    dx, dw, small = conv_bwd(dm, pooled, slope, padded, conv_weight, stitch_conv, per)
+    dw = lax.psum(dw, both)
+    cin, cout = conv_weight.shape[3:]
+    dw = dw.reshape(3, 2, cout, 3, cin).transpose(1, 0, 3, 4, 2)
+    small = lax.psum(small, both)
+    d_conv_bias = small[:, 0].reshape(2, cout)
+    d_stitch_conv = small[:, 128:130].T.reshape(2, 2, cout)
+    return stitched, dx, dw, d_conv_bias, d_stitch_conv, d_fc_weight, d_fc_bias, d_stitch_fc
+
+
+def shards(crop_pixels, live_rows, conv_weight, conv_bias, stitch_conv, fc_weight, fc_bias, stitch_fc, cotangent):
+    slots = crop_pixels.shape[0]
+    nb = lax.axis_size("batch")
+    b = lax.axis_index("batch")
+    fc = fc_weight.shape[2]
+    per = fc_weight.shape[1]
+    cols = fc // nb
+    both = ("batch", "tower")
+    feat, pooled, slope, padded = conv_fwd(live_rows, crop_pixels, conv_weight, conv_bias, stitch_conv, nb)
+    bias = lax.dynamic_slice_in_dim(fc_bias, b * cols, cols, axis=1)
+    mix = lax.dynamic_slice_in_dim(stitch_fc, b * cols, cols, axis=2).reshape(2, 2, 1, cols)
+    stitched, f, dh, dm, sums = fc_layer(feat, cotangent[0], fc_weight[0], bias, mix, nb, per)
+    d_fc_weight = lax.dot_general(f, dh, (((0,), (0,)), ((), ())), preferred_element_type=F32)[None]
+    d_stitch_fc = jnp.stack([sums[0, :2], sums[1, 1::-1]])
+    d_fc_bias = sums[:, 2]
+    dx, dw, small = conv_bwd(dm, pooled, slope, padded, conv_weight, stitch_conv, per)
     dw = lax.psum(dw, both)
     cin, cout = conv_weight.shape[3:]
     dw = dw.reshape(3, 2, cout, 3, cin).transpose(1, 0, 3, 4, 2)
@@ -254,4 +587,5 @@
         P("tower", "batch", None), P(("batch", "tower"), None, None, None), P(), P(), P(),
         P("tower", "batch", None), P(), P(),
     )
-    return jax.shard_map(shards, mesh=mesh, in_specs=in_specs, out_specs=out_specs, check_vma=False)
+    body = shards if mesh.shape["batch"] == 16 else plain_shards
+    return jax.shard_map(body, mesh=mesh, in_specs=in_specs, out_specs=out_specs, check_vma=False)

time: 581 us -> 399 us (0.69)
  Pallas kernels: 65.5 us -> 174 us
  blocking collectives: 108 us -> 0 us
  waiting for transfers between devices: 265 us -> 163 us
  other arithmetic: 43.3 us -> 0.66 us
  starting transfers between devices: 20.7 us -> 0.04 us
  matrix products: 18.1 us -> 5.34 us
    pallas_call x0 -> x1, Pallas kernels: none -> 108 us  [fc_layer(): pl.pallas_call(functools.partial(fc_kernel, parts, nb, per), out_shape=[j...]
    reduce_scatter x1 -> x0, waiting for transfers between devices: 73.7 us -> none  [shards(): hidden = lax.psum_scatter(part, 'batch', scatter_dimension=1, tiled=True)]
    all_gather x1 -> x0, waiting for transfers between devices: 65.4 us -> none  [shards(): dh = lax.all_gather(dh, 'batch', axis=1, tiled=True)]
    psum x1, waiting for transfers between devices: 112 us -> 163 us  [shards(): dw = lax.psum(dw, both)]
    all_gather x1 -> x0, blocking collectives: 46 us -> none  [shards(): lax.all_gather(sums, both, axis=0).reshape(nb, 2, 3, cols)]
    unnamed x1 -> x0, blocking collectives: 39.6 us -> none
    select_n x2 -> x0, other arithmetic: 31.8 us -> none  [the longest x1 31 us: shards(): jnp.where(slot % slots < counts[slot // slots], start[slot // slots] + sl...]
    all_to_all x1 -> x0, blocking collectives: 22.2 us -> none  [shards(): dm = lax.all_to_all(expand(df).reshape(2 * nb, slots, per), both, 0, 0)]
  transfers between devices with their start and end apart: 8 -> 1, of which waited for: 6 -> 1; matrix products, arithmetic and copies ran while one was open for 10% -> 3% of each run, Pallas kernels for 0% -> 0%
where the time goes in v2:
time: 399 us; the launch traced here: 397 us
  Pallas kernels  174 us (44%)
  waiting for transfers between devices  163 us (41%)
  local copies, waits for them, and re-layouts  39.4 us (10%)
  between operations  14.8 us (4%)
  matrix products  5.34 us (1%)
    psum x1, waiting for transfers between devices, shards(): dw = lax.psum(dw, both)  163 us
    pallas_call x1, Pallas kernels, fc_layer(): pl.pallas_call(functools.partial(fc_kernel, parts, nb, per), out_shape=[j...  108 us
    pallas_call x1, Pallas kernels, conv_bwd(): pl.pallas_call(conv_bwd_kernel, out_shape=[jax.ShapeDtypeStruct((slots, s...  42.4 us
    pallas_call x1, Pallas kernels, conv_fwd(): pl.pallas_call(functools.partial(conv_fwd_kernel, rows_per), out_shape=[j...  23.3 us
    unnamed x18, local copies, waits for them, and re-layouts  14.4 us
    reshape x1, local copies, waits for them, and re-layouts, shards(): dw = dw.reshape(3, 2, cout, 3, cin).transpose(1, 0, 3, 4, 2)  9.4 us
    pallas_call x1, local copies, waits for them, and re-layouts, conv_bwd(): pl.pallas_call(conv_bwd_kernel, out_shape=[jax.ShapeDtypeStruct((slots, s...  8.02 us
  transfers between devices with their start and end apart: 1, of which 1 were waited for; matrix products, arithmetic and copies ran while one was open for 3% of the time, Pallas kernels for 0%

profile of v2, /device:TPU:1, one launch (start us, length us, event | category | flops | bytes accessed | tf_op | source)
XLA Modules:
  0.0 397.2 jit_solution(6515936055100897667)
XLA Ops:
  7.2 0.0 copy-start
  7.2 0.0 all-reduce.3.cloned.1.call-start
  7.9 1.2 constant_dynamic-slice_fusion.1.bias_ref
  9.1 0.0 copy-done
  9.1 0.6 reshape.30.mix_ref
  9.7 3.6 copy.21.x_ref
  13.3 23.3 %shard_map.152 = (bf16[2,16,16,640]{3,2,1,0:T(8,128)(2,1)}, f32[36,16,512]{2,1,0:T(8,128)}, bf16[13,13,16,512]{3,2,1,0:T(8,128)(2,1)}, bf16[15,15,16,384]{3,2,1,0:T(8,128)(2,1)}) custom-call(s32[1]{0:T(128)S(6)} %copy.32.live_ref, bf16[16,13,13,384]{3,2,1,0:T(8,128)(2,1)} %copy.21.x_ref, bf16[2,3456,256]{2,1,0:T(8,128)(2,1)} %bitcast.17, f32[2,256]{1,0:T(2,128)} %b_ref.1, ...), custom_call_target="tpu_custom_call" | custom-call | tf_op jit(solution)/shard_map/pallas_call | solution.py:75
  36.6 108.5 %shard_map.153 = (bf16[1,32,4096]{2,1,0:T(8,128)(2,1)}, bf16[256,576]{1,0:T(8,128)(2,1)}, bf16[256,4096]{1,0:T(8,128)(2,1)}, bf16[2,16,16,640]{3,2,1,0:T(8,128)(2,1)}, f32[2,8,4096]{2,1,0:T(8,128)}) custom-call(bf16[2,16,16,640]{3,2,1,0:T(8,128)(2,1)} %get-tuple-element.20.feat_ref, bf16[32,4096]{1,0:T(8,128)(2,1)} %bitcast.21, bf16[576,4096]{1,0:T(8,128)(2,1)} %bitcast.19, ...), custom_call_target="tpu_custom_call" | custom-call | tf_op jit(solution)/shard_map/pallas_call | solution.py:375
  145.1 42.4 %shard_map.154 = (bf16[16,13,13,384]{3,2,1,0:T(8,128)(2,1)}, f32[3,512,1152]{2,1,0:T(8,128)}, f32[512,256]{1,0:T(8,128)}) custom-call(bf16[2,16,16,640]{3,2,1,0:T(8,128)(2,1)} %get-tuple-element.22.dm_ref, f32[36,16,512]{2,1,0:T(8,128)} %get-tuple-element.23.pooled_ref, bf16[13,13,16,512]{3,2,1,0:T(8,128)(2,1)} %get-tuple-element.24.slope_ref, ...), custom_call_target="tpu_custom_call" | custom-call | tf_op jit(solution)/shard_map/pallas_call | solution.py:478
  187.5 8.0 %copy.22 = f32[3,512,1152]{1,2,0:T(8,128)} copy(f32[3,512,1152]{2,1,0:T(8,128)} %get-tuple-element.27) | data formatting | bytes 14155776 | tf_op jit(solution)/shard_map/pallas_call | solution.py:478
  195.5 9.4 %reshape.31 = f32[3,2,256,3,384]{2,1,4,3,0:T(2,128)} reshape(f32[3,512,1152]{1,2,0:T(8,128)} %copy.22) | data formatting | bytes 14155776 | tf_op jit(solution)/shard_map/reshape | solution.py:574
  204.9 0.0 copy-start.2
  204.9 0.0 all-reduce.3.cloned.1.call-update
  204.9 0.0 copy-start.4
  204.9 1.1 slice.17
  206.1 0.6 copy.28
  206.7 1.0 fusion
  207.7 1.0 rev.3
  208.7 0.0 copy-start.3
  208.7 0.0 copy-done.2
  208.7 1.8 copy.23
  210.6 0.0 copy-done.4
  210.6 0.0 copy-done.3
  210.6 5.3 %convolution_bitcast_fusion = f32[1,576,4096]{2,1,0:T(8,128)} fusion(bf16[256,576]{1,0:T(8,128)(2,1)S(1)} %copy-done.4, bf16[256,4096]{1,0:T(8,128)(2,1)S(1)} %copy-done.3), kind=kOutput, calls=%fused_computation | convolution fusion | flops 1207959552 | bytes 11829248 | tf_op jit(solution)/shard_map/dot_general | solution.py:568
  215.9 0.7 pad_maximum_fusion
  216.6 162.8 %all-reduce.3.cloned.1.call-done = (f32[2,3,3,384,256]{4,0,3,2,1:T(2,128)}, f32[512,256]{1,0:T(8,128)}) async-done(((f32[2,3,3,384,256]{4,0,3,2,1:T(2,128)}, f32[512,256]{1,0:T(8,128)}), (f32[2,3,3,384,256]{4,0,3,2,1:T(2,128)}, f32[512,256]{1,0:T(8,128)})) %all-reduce.3.cloned.1.call-update) | async-done | bytes 7602192 | tf_op jit(solution)/shard_map/psum | solution.py:572
  379.3 1.1 slice_reduce_fusion
  380.4 1.0 slice.21
  381.4 0.0 copy-start.5
  381.4 0.0 copy-start.1
  381.4 6.9 %copy.24 = f32[2,3,3,384,256]{4,3,2,1,0:T(8,128)} copy(f32[2,3,3,384,256]{4,0,3,2,1:T(2,128)} %get-tuple-element.48) | data formatting | bytes 14155776
  388.3 0.7 copy.25
  389.0 0.6 reshape_squeeze.3
  389.6 0.0 copy-done.5
  389.6 0.7 copy.33
  390.3 0.0 copy-done.1
  (1 shorter events, 0.0 us)
Async XLA Ops:
  7.2 2.0 copy-start
  7.2 372.1 %all-reduce.3.cloned.1.call-start = ((), (), s32[]{:S(2)}) async-start(), calls=%async_computation | async-start | bytes 15204352 | tf_op jit(solution)/shard_map/psum | solution.py:572
  204.9 3.8 copy-start.2
  204.9 5.6 %copy-start.4 = (bf16[256,576]{1,0:T(8,128)(2,1)S(1)}, bf16[256,576]{1,0:T(8,128)(2,1)}, u32[]{:S(2)}) copy-start(bf16[256,576]{1,0:T(8,128)(2,1)} %get-tuple-element.29) | copy-start | bytes 884740
  208.7 1.8 copy-start.3
  381.4 8.2 %copy-start.5 = (bf16[1,32,4096]{2,1,0:T(8,128)(2,1)S(1)}, bf16[1,32,4096]{2,1,0:T(8,128)(2,1)}, u32[]{:S(2)}) copy-start(bf16[1,32,4096]{2,1,0:T(8,128)(2,1)} %get-tuple-element.60) | copy-start | bytes 786436
  381.4 8.9 %copy-start.1 = (f32[2,2,4096]{2,1,0:T(2,128)S(1)}, f32[2,2,4096]{2,1,0:T(2,128)}, u32[]{:S(2)}) copy-start(f32[2,2,4096]{2,1,0:T(2,128)} %param.16) | copy-start | bytes 196612
Sparse Core Ops, SparseCore 0:
  205.0 174.2 all-reduce.2

commit v3 on v2

--- a/solution.py
+++ b/solution.py
@@ -197,8 +197,8 @@
 
 
 def fc_kernel(parts, nb, per, feat_ref, cot_ref, w_hbm, bias_ref, mix_ref,
-              out_ref, f_ref, dh_ref, dm_ref, sums_ref,
-              w, fin, cin, cgot, spread, s, r1, t1, r2, t2, r3, g, keep, gates, cots, wide, st, sgot, dsl, acc,
+              out_ref, f_ref, g, dm_ref, sums_ref,
+              w, fin, cin, cgot, spread, s, r1, t1, r2, t2, r3, gates, cots, wide, st, sgot, dsl, acc,
               wsem, fs, fr, cs, cr, xs, xr, ss, sr, ms, mr, gs, gr):
     place = Place(nb)
     b, t = place.b, place.t
@@ -331,9 +331,6 @@
             device_id=(d // 2, d % 2), device_id_type=MESH_ID)
     lax.fori_loop(1, total, lambda k, _: (grad_copy(k).start(), 0)[1], 0)
     dm_ref[t, b] = dsl[me]
-    for k in range(nb):
-        i = (k // (place.dims[1] * place.dims[2]), (k // place.dims[2]) % place.dims[1], k % place.dims[2])
-        dh_ref[:, k * cols:(k + 1) * cols] = g[i]
     lax.fori_loop(1, nb, lambda k, _: (stitched_copy(k).wait_recv(), 0)[1], 0)
     for k in range(nb):
         out_ref[0, :, k * cols:(k + 1) * cols] = sgot[k]
@@ -375,19 +372,221 @@
     return pl.pallas_call(
         functools.partial(fc_kernel, parts, nb, per),
         out_shape=[jax.ShapeDtypeStruct((1, 2 * slots, fc), BF16), jax.ShapeDtypeStruct((live, per), BF16),
-                   jax.ShapeDtypeStruct((live, fc), BF16), jax.ShapeDtypeStruct((2, nb, slots, padded), BF16),
+                   jax.ShapeDtypeStruct((d0, d1, d2, live, cols), BF16), jax.ShapeDtypeStruct((2, nb, slots, padded), BF16),
                    jax.ShapeDtypeStruct((2, 8, fc), F32)],
         in_specs=[V, V, pl.BlockSpec(memory_space=pl.ANY), V, V], out_specs=[V] * 5,
         scratch_shapes=[
             vm(per, fc), vm(total, slots, padded), vm(nb, 2 * slots, cols), vm(nb, 2 * slots, cols), vm(rows, live),
             vm(d0, d1, d2, live, cols), vm(n, d1 - 1, d0, d1, size, cols), vm(n, d0, d1, size, cols),
-            vm(n, d1 - 1, d0, size, cols), vm(n, d0, size, cols), vm(n, d0 - 1, size, cols), vm(d0, d1, d2, live, cols),
-            vm(16, 128), vm(2, live, cols), vm(2, live, cols), pltpu.VMEM((total, 8, cols), F32),
+            vm(n, d1 - 1, d0, size, cols), vm(n, d0, size, cols), vm(n, d0 - 1, size, cols),
+            vm(2, live, cols), vm(2, live, cols), pltpu.VMEM((total, 8, cols), F32),
             vm(nb, 2 * slots, cols), vm(nb, 2 * slots, cols), vm(total, slots, padded), pltpu.VMEM((live, per), F32),
             pltpu.SemaphoreType.DMA, dma(2 * total), dma(2 * total), dma(nb), dma(nb), dma(2), dma(2), dma(nb), dma(nb),
             dma(total), dma(total), dma(n, hops(nb)), dma(n, hops(nb))],
         compiler_params=pltpu.CompilerParams(collective_id=1, has_side_effects=True, vmem_limit_bytes=60 * 2**20),
     )(feat, cot, w, bias, mix)
+
+def bwd_kernel(per, dm_ref, pooled_ref, slope_ref, p_ref, w_ref, mix_ref, dx_ref, out_ref,
+               fbuf, z, dpad, d2, dt, stage, keep, give, take, s, r1, t1, r2, t2, r3, cs, cr, gs, gr, stage_sums):
+    towers, nb, slots, _ = dm_ref.shape
+    place = Place(nb)
+    b, t = place.b, place.t
+    me = b * 2 + t
+    side = slope_ref.shape[0]
+    cout = w_ref.shape[2]
+    cin = p_ref.shape[3]
+    pool = (side - 3) // 2 + 1
+    wide = towers * cout
+    cells = side * side
+    chunks = out_ref.shape[1]
+    span = out_ref.shape[-1]
+    greet(nb, me)
+    for u in range(towers):
+        for k in range(nb):
+            fbuf[u, :, k * per:(k + 1) * per] = dm_ref[u, k, :, :per]
+    z[0] = jnp.zeros(z.shape[1:], F32)
+    z[pool + 1] = jnp.zeros(z.shape[1:], F32)
+    acc = [[jnp.zeros((slots, cout), F32)] * 2 for _ in range(2)]
+    for i in range(pool):
+        z[i + 1, 0] = jnp.zeros(z.shape[2:], F32)
+        z[i + 1, pool + 1] = jnp.zeros(z.shape[2:], F32)
+        for j in range(pool):
+            q = i * pool + j
+            dm = [fbuf[u, :, q * cout:(q + 1) * cout].astype(F32) for u in range(towers)]
+            for u in range(towers):
+                pu = pooled_ref[q, :, u * cout:(u + 1) * cout]
+                for v in range(towers):
+                    acc[v][u] = acc[v][u] + dm[v] * pu
+                z[i + 1, j + 1, :, u * cout:(u + 1) * cout] = (mix_ref[0, u][None] * dm[0] + mix_ref[1, u][None] * dm[1]) * (1.0 / 9.0)
+    sums = [jnp.concatenate([jnp.sum(acc[v][u], axis=0, keepdims=True) for u in range(2)], axis=1) for v in range(2)]
+    sums = jnp.concatenate([jnp.zeros((1, wide), F32)] + sums + [jnp.zeros((125, wide), F32)], axis=0).T
+    dpad[0] = jnp.zeros(dpad.shape[1:], BF16)
+    dpad[side + 1] = jnp.zeros(dpad.shape[1:], BF16)
+    d2[cells:] = jnp.zeros((d2.shape[0] - cells, slots, wide), BF16)
+    def drow(y, src):
+        dpad[y + 1, 0] = jnp.zeros((slots, wide), BF16)
+        dpad[y + 1, side + 1] = jnp.zeros((slots, wide), BF16)
+        for x in range(side):
+            j = x // 2
+            v = src(j + 1) if x % 2 else src(j) + src(j + 1)
+            d = (v * slope_ref[y, x].astype(F32)).astype(BF16)
+            dpad[y + 1, x + 1] = d
+            d2[y * side + x] = d
+    def pair(i, _):
+        drow(2 * i, lambda j: z[i, j] + z[i + 1, j])
+        drow(2 * i + 1, lambda j: z[i + 1, j])
+        return 0
+    lax.fori_loop(0, pool, pair, 0)
+    drow(side - 1, lambda j: z[pool, j] + z[pool + 1, j])
+    step = 256 // slots
+    def flip(k, _):
+        dt[:, pl.ds(pl.multiple_of(k * 256, 256), 256)] = d2[pl.ds(k * step, step)].reshape(256, wide).T
+        return 0
+    lax.fori_loop(0, d2.shape[0] // step, flip, 0)
+    depth = dt.shape[1]
+    tail = depth - cells * slots
+    other = (b, 1 - t)
+
+    def window(n):
+        cols = []
+        low = n * span
+        while low < (n + 1) * span:
+            k = low // cin
+            if k < 9:
+                high = min((n + 1) * span, (k + 1) * cin)
+                a, c = k // 3, k % 3
+                cols.append(p_ref[a:a + side, c:c + side, :, low - k * cin:high - k * cin].reshape(cells * slots, high - low))
+                low = high
+            else:
+                cols.append(jnp.ones((cells * slots, (n + 1) * span - low), BF16))
+                low = (n + 1) * span
+        win = cols[0] if len(cols) == 1 else jnp.concatenate(cols, axis=1)
+        return jnp.concatenate([win, jnp.zeros((tail, span), BF16)], axis=0)
+
+    pieces = [Sum(place, 2 - n % 2, s.at[n], r1.at[n], t1.at[n], r2.at[n], t2.at[n], r3.at[n], out_ref.at[t, n], gs.at[n], gr.at[n])
+              for n in range(chunks)]
+    core = {}
+
+    def compute(n):
+        win = window(n)
+        def half(u):
+            v = jnp.dot(dt[pl.ds(pl.multiple_of(u * cout, cout), cout), :], win, preferred_element_type=F32)
+            if n == chunks - 1:
+                rows = stage_sums[pl.ds(pl.multiple_of(u * cout, cout), cout), :]
+                lane = lax.broadcasted_iota(jnp.int32, rows.shape, 1)
+                v = jnp.concatenate([v[:, :span - 128], jnp.where(lane == 0, v[:, span - 128:], rows)], axis=1)
+            return v
+        give[n] = half(1 - t).astype(BF16)
+        core[n] = send(give.at[n], take.at[n], cs.at[n, 0], cr.at[n, 0], other)
+        keep[n % keep.shape[0]] = half(t)
+
+    stage_sums[...] = sums
+
+    def merge(n):
+        core[n].wait_recv()
+        s[n] = (keep[n % keep.shape[0]] + take[n].astype(F32)).astype(BF16).reshape(s.shape[1:])
+        pieces[n].send1()
+
+    def finish(n):
+        out_ref[t, n, place.at[0], place.at[1], place.at[2]] = pieces[n].result().astype(BF16)
+        pieces[n].gather1()
+
+    back = {}
+    def share(n):
+        pieces[n].arrive()
+        back[n] = send(out_ref.at[t, n], out_ref.at[t, n], cs.at[n, 1], cr.at[n, 1], other)
+
+    pitch = 16
+    def xrow(y):
+        lhs = jnp.concatenate([dpad[y + 2 - a, 2 - c:2 - c + side, :, u * cout:(u + 1) * cout].reshape(side * slots, cout)
+                               for u in range(towers) for a in range(3) for c in range(3)], axis=1)
+        rhs = jnp.concatenate([w_ref[u, (a * 3 + c) * cin:(a * 3 + c + 1) * cin, :]
+                               for u in range(towers) for a in range(3) for c in range(3)], axis=1)
+        out = lax.dot_general(lhs, rhs, (((1,), (1,)), ((), ())), preferred_element_type=F32).reshape(side, slots, cin)
+        for x in range(side):
+            for l in range(cin // 128):
+                stage[l, pl.ds(y * pitch + x, slots, stride=side * pitch), :] = out[x, :, l * 128:(l + 1) * 128]
+
+    work = [merge, lambda n: pieces[n].send2(), lambda n: pieces[n].send3(), finish,
+            lambda n: pieces[n].gather2(), lambda n: pieces[n].gather3(), share, lambda n: back[n].wait_recv()]
+    rows_left = list(range(side))
+    for step in range(chunks + 3 * (len(work) - 1) + 1):
+        if step < chunks:
+            compute(step)
+        if step >= 14 and rows_left:
+            xrow(rows_left.pop(0))
+        for k, job in enumerate(work):
+            n = step - 1 - 3 * k
+            if 0 <= n < chunks:
+                job(n)
+    for y in rows_left:
+        xrow(y)
+    def put(k, _):
+        r = k // side
+        i = k % side
+        dx_ref[r, i] = jnp.concatenate([stage[l, pl.ds(pl.multiple_of(k * pitch, pitch), side), :] for l in range(cin // 128)], axis=1).astype(BF16)
+        return 0
+    lax.fori_loop(0, slots * side, put, 0, unroll=4)
+    for n in range(chunks):
+        pieces[n].close()
+        core[n].wait_send()
+        back[n].wait_send()
+
+
+def bwd_layer(dm, pooled, slope, p, w, mix, per):
+    towers, nb, slots, _ = dm.shape
+    side = slope.shape[0]
+    cin = p.shape[3]
+    cout = w.shape[4]
+    pool = (side - 3) // 2 + 1
+    wide = towers * cout
+    span = 256
+    chunks = (9 * cin + 128) // span
+    d0, d1, d2 = torus(nb)
+    V = pl.BlockSpec(memory_space=pltpu.VMEM)
+    vm = lambda *shape: pltpu.VMEM(shape, BF16)
+    dma = lambda *shape: pltpu.SemaphoreType.DMA(shape)
+    cells = -(-side * side * slots // 256) * 256 // slots
+    h = cout // nb
+    return pl.pallas_call(
+        functools.partial(bwd_kernel, per),
+        out_shape=[jax.ShapeDtypeStruct((slots, side, side, cin), BF16),
+                   jax.ShapeDtypeStruct((towers, chunks, d0, d1, d2, h, span), BF16)],
+        in_specs=[V] * 6, out_specs=[V] * 2,
+        scratch_shapes=[vm(towers, slots, nb * per), pltpu.VMEM((pool + 2, pool + 2, slots, wide), F32),
+                        vm(side + 2, side + 2, slots, wide), vm(cells, slots, wide), vm(wide, cells * slots),
+                        pltpu.VMEM((cin // 128, slots * side * 16, 128), F32), pltpu.VMEM((2, cout, span), F32),
+                        vm(chunks, cout, span), vm(chunks, cout, span),
+                        vm(chunks, d0, d1, d2, h, span), vm(chunks, d1 - 1, d0, d1, h, span), vm(chunks, d0, d1, h, span),
+                        vm(chunks, d1 - 1, d0, h, span), vm(chunks, d0, h, span), vm(chunks, d0 - 1, h, span),
+                        dma(chunks, 2), dma(chunks, 2), dma(chunks, hops(nb)), dma(chunks, hops(nb)), pltpu.VMEM((wide, 128), F32)],
+        compiler_params=pltpu.CompilerParams(collective_id=2, has_side_effects=True, vmem_limit_bytes=62 * 2**20),
+    )(dm, pooled, slope, p, w.reshape(towers, 9 * cin, cout), mix)
+
+
+def write_kernel(taps, f_ref, g_ref, dw_ref, fc_ref, conv_ref):
+    k = pl.program_id(0)
+    fc_ref[0] = lax.dot_general(f_ref[...], g_ref[0], (((0,), (0,)), ((), ())), preferred_element_type=F32)
+    conv_ref[0] = dw_ref[0, 0].astype(F32).T
+    if taps > 1:
+        conv_ref[1] = dw_ref[1, 0].astype(F32).T
+
+
+def write_grads(f, g, dw, nb, cols, ktaps):
+    live, per = f.shape
+    towers, chunks, cout, span = dw.shape
+    last = chunks - 1
+    return pl.pallas_call(
+        functools.partial(write_kernel, towers),
+        grid=(nb,),
+        out_shape=[jax.ShapeDtypeStruct((1, per, nb * cols), F32), jax.ShapeDtypeStruct((towers, ktaps, cout), F32)],
+        in_specs=[pl.BlockSpec((live, per), lambda k: (0, 0)), pl.BlockSpec((1, live, cols), lambda k: (k, 0, 0)),
+                  pl.BlockSpec((towers, 1, cout, span), lambda k: (0, jnp.minimum(k, last), 0, 0))],
+        out_specs=[pl.BlockSpec((1, per, cols), lambda k: (0, 0, k)),
+                   pl.BlockSpec((towers, span, cout), lambda k: (0, jnp.minimum(k, last), 0))],
+        compiler_params=pltpu.CompilerParams(vmem_limit_bytes=32 * 2**20),
+    )(f, g, dw)
+
 
 def conv_bwd_kernel(dm_ref, pooled_ref, slope_ref, p_ref, w_ref, mix_ref, dx_ref, dw_ref, small_ref,
                     fbuf, z, dpad, d2, dt, stage):
@@ -560,22 +759,21 @@
     fc = fc_weight.shape[2]
     per = fc_weight.shape[1]
     cols = fc // nb
-    both = ("batch", "tower")
+    cin, cout = conv_weight.shape[3:]
+    live = slots * nb
     feat, pooled, slope, padded = conv_fwd(live_rows, crop_pixels, conv_weight, conv_bias, stitch_conv, nb)
     bias = lax.dynamic_slice_in_dim(fc_bias, b * cols, cols, axis=1)
     mix = lax.dynamic_slice_in_dim(stitch_fc, b * cols, cols, axis=2).reshape(2, 2, 1, cols)
     stitched, f, dh, dm, sums = fc_layer(feat, cotangent[0], fc_weight[0], bias, mix, nb, per)
-    d_fc_weight = lax.dot_general(f, dh, (((0,), (0,)), ((), ())), preferred_element_type=F32)[None]
     d_stitch_fc = jnp.stack([sums[0, :2], sums[1, 1::-1]])
     d_fc_bias = sums[:, 2]
-    dx, dw, small = conv_bwd(dm, pooled, slope, padded, conv_weight, stitch_conv, per)
-    dw = lax.psum(dw, both)
-    cin, cout = conv_weight.shape[3:]
-    dw = dw.reshape(3, 2, cout, 3, cin).transpose(1, 0, 3, 4, 2)
-    small = lax.psum(small, both)
-    d_conv_bias = small[:, 0].reshape(2, cout)
-    d_stitch_conv = small[:, 128:130].T.reshape(2, 2, cout)
-    return stitched, dx, dw, d_conv_bias, d_stitch_conv, d_fc_weight, d_fc_bias, d_stitch_fc
+    dx, dw = bwd_layer(dm, pooled, slope, padded, conv_weight, stitch_conv, per)
+    dw = dw.reshape(2, dw.shape[1], cout, dw.shape[-1])
+    d_fc_weight, d_kernel = write_grads(f, dh.reshape(nb, live, cols), dw, nb, cols, 9 * cin)
+    small = dw[:, -1, :, 128:131].astype(F32)
+    d_conv_bias = small[:, :, 0]
+    d_stitch_conv = small[:, :, 1:].transpose(2, 0, 1)
+    return stitched, dx, d_kernel.reshape(conv_weight.shape), d_conv_bias, d_stitch_conv, d_fc_weight, d_fc_bias, d_stitch_fc
 
 
 def solution(mesh):

time: 399 us -> 237 us (0.59)
  waiting for transfers between devices: 163 us -> 0 us
  Pallas kernels: 174 us -> 217 us
  local copies, waits for them, and re-layouts: 39.4 us -> 16.8 us
  between operations: 14.8 us -> 1.39 us
  matrix products: 5.34 us -> 0 us
    psum x1 -> x0, waiting for transfers between devices: 163 us -> none  [shards(): dw = lax.psum(dw, both)]
    pallas_call x1 -> x2, Pallas kernels: 42.4 us -> 85.2 us  [the longest x1 74.7 us: bwd_layer(): pl.pallas_call(functools.partial(bwd_kernel, per), out_shape=[jax.ShapeDt...]
    reshape x1 -> x0, local copies, waits for them, and re-layouts: 9.4 us -> none  [shards(): dw = dw.reshape(3, 2, cout, 3, cin).transpose(1, 0, 3, 4, 2)]
    pallas_call x1 -> x0, local copies, waits for them, and re-layouts: 8.02 us -> none  [conv_bwd(): pl.pallas_call(conv_bwd_kernel, out_shape=[jax.ShapeDtypeStruct((slots, s...]
    dot_general x1 -> x0, matrix products: 5.34 us -> none  [shards(): lax.dot_general(f, dh, (((0,), (0,)), ((), ())), preferred_element_type=F32)]
    unnamed x18 -> x15, local copies, waits for them, and re-layouts: 14.4 us -> 11.4 us
  transfers between devices with their start and end apart: 1 -> 0, of which waited for: 1 -> 0; matrix products, arithmetic and copies ran while one was open for 3% -> 0% of each run, Pallas kernels for 0% -> 0%
where the time goes in v3:
time: 237 us
  Pallas kernels  217 us (92%)
  local copies, waits for them, and re-layouts  16.8 us (7%)
    pallas_call x1, Pallas kernels, fc_layer(): pl.pallas_call(functools.partial(fc_kernel, parts, nb, per), out_shape=[j...  108 us
    pallas_call x1, Pallas kernels, bwd_layer(): pl.pallas_call(functools.partial(bwd_kernel, per), out_shape=[jax.ShapeDt...  74.7 us
    pallas_call x1, Pallas kernels, conv_fwd(): pl.pallas_call(functools.partial(conv_fwd_kernel, rows_per), out_shape=[j...  23.3 us
    unnamed x15, local copies, waits for them, and re-layouts  11.4 us
    pallas_call x1, Pallas kernels, write_grads(): pl.pallas_call(functools.partial(write_kernel, towers), grid=(nb,), out_s...  10.5 us

profile of v3, /device:TPU:1, one launch (start us, length us, event | category | flops | bytes accessed | tf_op | source)
XLA Modules:
  0.0 236.7 jit_solution(8357620211329122329)
XLA Ops:
  0.6 0.0 copy-start
  1.3 1.2 constant_dynamic-slice_fusion.1.bias_ref
  2.6 0.0 copy-done
  2.6 0.6 reshape.35.mix_ref
  3.2 3.6 %copy.20.x_ref = bf16[16,13,13,384]{3,2,1,0:T(8,128)(2,1)} copy(bf16[16,13,13,384]{3,0,2,1:T(8,128)(2,1)} %param.9) | data formatting | bytes 4153344 | tf_op args[0]
  6.8 23.3 %shard_map.152 = (bf16[2,16,16,640]{3,2,1,0:T(8,128)(2,1)}, f32[36,16,512]{2,1,0:T(8,128)}, bf16[13,13,16,512]{3,2,1,0:T(8,128)(2,1)}, bf16[15,15,16,384]{3,2,1,0:T(8,128)(2,1)}) custom-call(s32[1]{0:T(128)S(6)} %copy.27.live_ref, bf16[16,13,13,384]{3,2,1,0:T(8,128)(2,1)} %copy.20.x_ref, bf16[2,3456,256]{2,1,0:T(8,128)(2,1)} %bitcast.19, f32[2,256]{1,0:T(2,128)} %b_ref.1, ...), custom_call_target="tpu_custom_call" | custom-call | tf_op jit(solution)/shard_map/pallas_call | solution.py:75
  30.1 108.4 %shard_map.153 = (bf16[1,32,4096]{2,1,0:T(8,128)(2,1)}, bf16[256,576]{1,0:T(8,128)(2,1)}, bf16[4,2,2,256,256]{4,3,2,1,0:T(8,128)(2,1)}, bf16[2,16,16,640]{3,2,1,0:T(8,128)(2,1)}, f32[2,8,4096]{2,1,0:T(8,128)}) custom-call(bf16[2,16,16,640]{3,2,1,0:T(8,128)(2,1)} %get-tuple-element.21.feat_ref, bf16[32,4096]{1,0:T(8,128)(2,1)} %bitcast.22, ...), custom_call_target="tpu_custom_call" | custom-call | tf_op jit(solution)/shard_map/pallas_call | solution.py:372
  138.5 74.7 %shard_map.154 = (bf16[16,13,13,384]{3,2,1,0:T(8,128)(2,1)}, bf16[2,14,4,2,2,16,256]{6,5,4,3,2,1,0:T(8,128)(2,1)}) custom-call(bf16[2,16,16,640]{3,2,1,0:T(8,128)(2,1)} %get-tuple-element.23.dm_ref, f32[36,16,512]{2,1,0:T(8,128)} %get-tuple-element.24.pooled_ref, bf16[13,13,16,512]{3,2,1,0:T(8,128)(2,1)} %get-tuple-element.25.slope_ref, ...), custom_call_target="tpu_custom_call" | custom-call | tf_op jit(solution)/shard_map/pallas_call | solution.py:551
  213.2 0.0 copy-start.2
  213.2 0.0 copy-start.3
  213.2 3.7 %copy.21 = bf16[16,13,13,384]{3,0,2,1:T(8,128)(2,1)} copy(bf16[16,13,13,384]{3,2,1,0:T(8,128)(2,1)} %get-tuple-element.43) | data formatting | bytes 4153344
  216.9 1.0 slice.21
  217.9 1.0 fusion.1
  218.9 0.6 copy.25
  219.5 0.8 rev.3
  220.3 0.7 pad_maximum_fusion
  221.0 0.9 fusion
  221.9 0.7 slice_reduce_fusion
  222.6 0.1 slice_bitcast_fusion
  222.8 0.7 copy.22
  223.5 0.0 copy-done.2
  223.5 0.0 copy-done.3
  223.5 0.0 copy-start.1
  223.5 2.0 copy-done.1
  225.5 0.0 copy-start.4
  225.5 10.5 %shard_map.155 = (f32[1,576,4096]{2,1,0:T(8,128)}, f32[2,3456,256]{2,1,0:T(8,128)}) custom-call(bf16[256,576]{1,0:T(8,128)(2,1)S(1)} %copy-done.3, bf16[16,256,256]{2,1,0:T(8,128)(2,1)S(1)} %bitcast.18, bf16[2,14,256,256]{3,2,1,0:T(8,128)(2,1)S(1)} %bitcast.17), custom_call_target="tpu_custom_call" | custom-call | tf_op jit(solution)/shard_map/pallas_call | solution.py:579
  236.0 0.0 copy-done.4
  236.0 0.7 copy.28
  (1 shorter events, 0.0 us)
Async XLA Ops:
  0.6 1.9 copy-start
  213.2 10.2 %copy-start.2 = (bf16[4,2,2,256,256]{4,3,2,1,0:T(8,128)(2,1)S(1)}, bf16[4,2,2,256,256]{4,3,2,1,0:T(8,128)(2,1)}, u32[]{:S(2)}) copy-start(bf16[4,2,2,256,256]{4,3,2,1,0:T(8,128)(2,1)} %get-tuple-element.29) | copy-start | bytes 6291460
  213.2 10.2 %copy-start.3 = (bf16[256,576]{1,0:T(8,128)(2,1)S(1)}, bf16[256,576]{1,0:T(8,128)(2,1)}, u32[]{:S(2)}) copy-start(bf16[256,576]{1,0:T(8,128)(2,1)} %get-tuple-element.28.f_ref) | copy-start | bytes 884740
  223.5 2.0 copy-start.1
  225.5 10.5 %copy-start.4 = (bf16[1,32,4096]{2,1,0:T(8,128)(2,1)S(1)}, bf16[1,32,4096]{2,1,0:T(8,128)(2,1)}, u32[]{:S(2)}) copy-start(bf16[1,32,4096]{2,1,0:T(8,128)(2,1)} %get-tuple-element.60) | copy-start | bytes 786436

commit v4 on v1

--- a/solution.py
+++ b/solution.py
@@ -15,7 +15,7 @@
     slope = half + value * (1.0 - half) * (2.0 * CG + (6.0 * CG * 0.044715) * sq)
     return value, slope
 
-def conv_fwd_kernel(rows_per, x_ref, w_ref, b_ref, mix_ref, feat_ref, pooled_ref, slope_ref, p_ref, stage, act, fbuf):
+def conv_fwd_kernel(rows_per, live_ref, x_ref, w_ref, b_ref, mix_ref, feat_ref, pooled_ref, slope_ref, p_ref, stage, act, fbuf):
     slots, side, _, cin = x_ref.shape
     towers, _, cout = w_ref.shape
     pool = (side - 3) // 2 + 1
@@ -58,12 +58,15 @@
             for t in range(towers):
                 m = mix_ref[t, 0][None] * p9[:, :cout] + mix_ref[t, 1][None] * p9[:, cout:]
                 fbuf[t, :, (i * pool + j) * cout:(i * pool + j + 1) * cout] = m.astype(BF16)
-    nb, per = feat_ref.shape[1], feat_ref.shape[3]
+    nb = feat_ref.shape[1]
+    per = fbuf.shape[2] // nb
+    flags = (lax.broadcasted_iota(jnp.int32, (slots, feat_ref.shape[3] - per), 0) < live_ref[0]).astype(F32).astype(BF16)
     for t in range(towers):
         for b in range(nb):
-            feat_ref[t, b] = fbuf[t, :, b * per:(b + 1) * per]
-
-def conv_fwd(x, w, bias, mix, nb, rows_per=1):
+            feat_ref[t, b, :, :per] = fbuf[t, :, b * per:(b + 1) * per]
+            feat_ref[t, b, :, per:] = flags
+
+def conv_fwd(live, x, w, bias, mix, nb, rows_per=1):
     slots, side, _, cin = x.shape
     towers, _, _, _, cout = w.shape
     pool = (side - 3) // 2 + 1
@@ -71,20 +74,121 @@
     V = pl.BlockSpec(memory_space=pltpu.VMEM)
     return pl.pallas_call(
         functools.partial(conv_fwd_kernel, rows_per),
-        out_shape=[jax.ShapeDtypeStruct((towers, nb, slots, nf // nb), BF16),
+        out_shape=[jax.ShapeDtypeStruct((towers, nb, slots, nf // nb // 128 * 128 + 128), BF16),
                    jax.ShapeDtypeStruct((pool * pool, slots, towers * cout), F32),
                    jax.ShapeDtypeStruct((side, side, slots, towers * cout), BF16),
                    jax.ShapeDtypeStruct((side + 2, side + 2, slots, cin), BF16)],
-        in_specs=[V] * 4, out_specs=[V] * 4,
+        in_specs=[pl.BlockSpec(memory_space=pltpu.SMEM)] + [V] * 4, out_specs=[V] * 4,
         scratch_shapes=[pltpu.VMEM((cin // 128, slots * side * 16, 128), F32),
                         pltpu.VMEM((side, side, slots, towers * cout), F32),
                         pltpu.VMEM((towers, slots, nf), BF16)],
         compiler_params=pltpu.CompilerParams(vmem_limit_bytes=60 * 2**20),
-    )(x, w.reshape(towers, 9 * cin, cout), bias, mix)
+    )(live, x, w.reshape(towers, 9 * cin, cout), bias, mix)
+
+
+MESH_ID = pl.DeviceIdType.MESH
+
+
+def torus(nb):
+    return {16: (4, 2, 2), 64: (4, 4, 4)}.get(nb, (nb, 1, 1))
+
+
+class Place:
+    def __init__(self, nb):
+        self.dims = torus(nb)
+        self.b, self.t = lax.axis_index("batch"), lax.axis_index("tower")
+        d0, d1, d2 = self.dims
+        self.at = (self.b // (d1 * d2), (self.b // d2) % d1, self.b % d2)
+
+    def peer(self, dim, k):
+        c = list(self.at)
+        c[dim] = k
+        return ((c[0] * self.dims[1] + c[1]) * self.dims[2] + c[2], self.t)
+
+
+def send(src, dst, ssem, rsem, device):
+    copy = pltpu.make_async_remote_copy(src_ref=src, dst_ref=dst, send_sem=ssem, recv_sem=rsem, device_id=device, device_id_type=MESH_ID)
+    copy.start()
+    return copy
+
+
+class Sum:
+    def __init__(self, place, p, s, r1, t1, r2, t2, r3, g, ssem, rsem):
+        self.place, self.p, self.q = place, p, 3 - p
+        self.s, self.r1, self.t1, self.r2, self.t2, self.r3, self.g = s, r1, t1, r2, t2, r3, g
+        self.ssem, self.rsem = ssem, rsem
+        self.sent = []
+        self.used = 0
+
+    def pick(self, ref, k):
+        return ref.at[:, :, k] if self.p == 2 else ref.at[:, k]
+
+    def post(self, dim, src_of, dst_of):
+        n = self.place.dims[dim]
+        self.flight = []
+        for j in range(1, n):
+            k = lax.rem(self.place.at[dim] + j, n)
+            i = self.used
+            self.used += 1
+            self.flight.append(send(src_of(k), dst_of(j - 1), self.ssem.at[i], self.rsem.at[i], self.place.peer(dim, k)))
+        self.sent += self.flight
+
+    def arrive(self):
+        for c in self.flight:
+            c.wait_recv()
+
+    def add(self, mine, got, n):
+        v = mine.astype(F32)
+        for j in range(n):
+            v = v + got[j].astype(F32)
+        return v
+
+    def send1(self):
+        self.post(self.p, lambda k: self.pick(self.s, k), lambda j: self.r1.at[j])
+
+    def send2(self):
+        self.arrive()
+        n = self.place.dims[self.p]
+        self.t1[...] = self.add(self.pick(self.s, self.place.at[self.p])[...], self.r1, n - 1).astype(BF16)
+        self.post(self.q, lambda k: self.t1.at[:, k], lambda j: self.r2.at[j])
+
+    def send3(self):
+        self.arrive()
+        n = self.place.dims[self.q]
+        self.t2[...] = self.add(self.t1[:, self.place.at[self.q]], self.r2, n - 1).astype(BF16)
+        self.post(0, lambda k: self.t2.at[k], lambda j: self.r3.at[j])
+
+    def result(self):
+        self.arrive()
+        return self.add(self.t2[self.place.at[0]], self.r3, self.place.dims[0] - 1)
+
+    def gather1(self):
+        mine = self.g.at[self.place.at[0], self.place.at[1], self.place.at[2]]
+        self.post(0, lambda k: mine, lambda j: mine)
+
+    def gather2(self):
+        self.arrive()
+        mine = self.g.at[:, self.place.at[1], self.place.at[2]]
+        self.post(self.q, lambda k: mine, lambda j: mine)
+
+    def gather3(self):
+        self.arrive()
+        mine = self.pick(self.g, self.place.at[self.p])
+        self.post(self.p, lambda k: mine, lambda j: mine)
+
+    def close(self):
+        for c in self.sent:
+            c.wait_send()
+
+
+def hops(nb):
+    return 2 * sum(d - 1 for d in torus(nb))
+
 
 def conv_bwd_kernel(dm_ref, pooled_ref, slope_ref, p_ref, w_ref, mix_ref, dx_ref, dw_ref, small_ref,
                     fbuf, z, dpad, d2, dt, stage):
-    towers, nb, slots, per = dm_ref.shape
+    towers, nb, slots, _ = dm_ref.shape
+    per = fbuf.shape[2] // nb
     side = slope_ref.shape[0]
     cout = w_ref.shape[2]
     cin = p_ref.shape[3]
@@ -93,7 +197,7 @@
     cells = side * side
     for t in range(towers):
         for b in range(nb):
-            fbuf[t, :, b * per:(b + 1) * per] = dm_ref[t, b]
+            fbuf[t, :, b * per:(b + 1) * per] = dm_ref[t, b, :, :per]
     z[0] = jnp.zeros(z.shape[1:], F32)
     z[pool + 1] = jnp.zeros(z.shape[1:], F32)
     acc = [[jnp.zeros((slots, cout), F32)] * 2 for _ in range(2)]
@@ -158,8 +262,8 @@
         return 0
     lax.fori_loop(0, slots * side, put, 0, unroll=4)
 
-def conv_bwd(dm, pooled, slope, p, w, mix):
-    towers, nb, slots, per = dm.shape
+def conv_bwd(dm, pooled, slope, p, w, mix, per):
+    towers, nb, slots, _ = dm.shape
     side = slope.shape[0]
     cin = p.shape[3]
     cout = w.shape[4]
@@ -187,7 +291,7 @@
     return lax.ppermute(block, "tower", [(0, 1), (1, 0)])
 
 
-def shards(crop_pixels, live_rows, conv_weight, conv_bias, stitch_conv, fc_weight, fc_bias, stitch_fc, cotangent):
+def plain_shards(crop_pixels, live_rows, conv_weight, conv_bias, stitch_conv, fc_weight, fc_bias, stitch_fc, cotangent):
     slots = crop_pixels.shape[0]
     nb = lax.axis_size("batch")
     b, t = lax.axis_index("batch"), lax.axis_index("tower")
@@ -197,10 +301,10 @@
     per = fc_weight.shape[1]
     cols = fc // nb
     w = fc_weight[0]
-    feat, pooled, slope, padded = conv_fwd(crop_pixels, conv_weight, conv_bias, stitch_conv, nb)
+    feat, pooled, slope, padded = conv_fwd(live_rows, crop_pixels, conv_weight, conv_bias, stitch_conv, nb)
     both = ("batch", "tower")
     counts = lax.all_gather(live_rows, both, axis=0, tiled=True)
-    got = lax.all_to_all(feat.transpose(1, 0, 2, 3).reshape(2 * nb, slots, per), both, 0, 0).reshape(rows, per)
+    got = lax.all_to_all(feat[..., :per].transpose(1, 0, 2, 3).reshape(2 * nb, slots, per), both, 0, 0).reshape(rows, per)
     slot = jnp.arange(rows, dtype=jnp.int32)
     start = jnp.cumsum(counts) - counts
     place = jnp.where(slot % slots < counts[slot // slots], start[slot // slots] + slot % slots, -1)
@@ -235,7 +339,7 @@
     df = lax.dot_general(dh, w, (((1,), (1,)), ((), ())), preferred_element_type=F32).astype(BF16)
     dm = lax.all_to_all(expand(df).reshape(2 * nb, slots, per), both, 0, 0)
     dm = dm.reshape(nb, 2, slots, per).transpose(1, 0, 2, 3)
-    dx, dw, small = conv_bwd(dm, pooled, slope, padded, conv_weight, stitch_conv)
+    dx, dw, small = conv_bwd(dm, pooled, slope, padded, conv_weight, stitch_conv, per)
     dw = lax.psum(dw, both)
     cin, cout = conv_weight.shape[3:]
     dw = dw.reshape(3, 2, cout, 3, cin).transpose(1, 0, 3, 4, 2)
@@ -243,6 +347,478 @@
     d_conv_bias = small[:, 0].reshape(2, cout)
     d_stitch_conv = small[:, 128:130].T.reshape(2, 2, cout)
     return stitched, dx, dw, d_conv_bias, d_stitch_conv, d_fc_weight, d_fc_bias, d_stitch_fc
+
+
+def whole_kernel(parts, per, live_ref, x_hbm, cw_hbm, cbias_ref, cmix_ref, cot_ref, w_hbm, bias_ref, fmix_ref,
+                 out_ref, dx_hbm, f_ref, g, grad_ref, stitch_ref, fbias_ref,
+                 xin, cw, stage, act, p, slope, pooled, fbuf, feat, fin, dm, w, cin, cgot, sgot, spread,
+                 s, r1, t1, r2, t2, r3, gates, cots, wide, acc,
+                 z, dpad, d2, dt, keep, cs_, cr1, ct1, cr2, ct2, cr3, sums_t,
+                 xsem, lsem, wsem, fs, fr, cs, cr, xs, xr, ss, sr, ms, mr, gs, gr, ds, dr, ks, kr, hs, hr):
+    nb = cin.shape[0]
+    place = Place(nb)
+    b, t = place.b, place.t
+    me = b * 2 + t
+    total = 2 * nb
+    slots, side, _, chan = xin.shape
+    towers, _, cout = cw.shape
+    pool = (side - 3) // 2 + 1
+    wide_c = towers * cout
+    pitch = 16
+    lanes = chan // 128
+    padded = feat.shape[2]
+    rows = total * slots
+    live = rows // 2
+    cols = cin.shape[2]
+    other = (b, 1 - t)
+    device = lambda d: (d // 2, d % 2)
+
+    groups = xsem.shape[0]
+    crops = slots // groups
+    loads = [pltpu.make_async_copy(x_hbm.at[pl.ds(k * crops, crops)], xin.at[pl.ds(k * crops, crops)], xsem.at[k]) for k in range(groups)]
+    for c in loads:
+        c.start()
+    cw_load = pltpu.make_async_copy(cw_hbm, cw, lsem)
+    cw_load.start()
+    w_loads = [pltpu.make_async_copy(w_hbm.at[:, pl.ds(k * cols, cols)], w.at[k], wsem.at[k]) for k in range(nb)]
+    for c in w_loads:
+        c.start()
+    bar = pltpu.get_barrier_semaphore()
+    def hail(k, _):
+        pl.semaphore_signal(bar, inc=1, device_id=device(lax.rem(me + k, total)), device_id_type=MESH_ID)
+        return 0
+    lax.fori_loop(1, total, hail, 0)
+    for k in range(nb):
+        cin[k] = cot_ref[:, k * cols:(k + 1) * cols]
+    cgot[b] = cin[b]
+
+    p[0] = jnp.zeros(p.shape[1:], BF16)
+    p[side + 1] = jnp.zeros(p.shape[1:], BF16)
+    for q in range(groups):
+        loads[q].wait()
+        def put(k, _):
+            v = xin[k // side, k % side].astype(F32)
+            for l in range(lanes):
+                stage[l, pl.ds(pl.multiple_of(k * pitch, pitch), side), :] = v[:, l * 128:(l + 1) * 128]
+            return 0
+        lax.fori_loop(q * crops * side, (q + 1) * crops * side, put, 0, unroll=4)
+    def take_row(i, _):
+        p[i + 1, 0] = jnp.zeros((slots, chan), BF16)
+        p[i + 1, side + 1] = jnp.zeros((slots, chan), BF16)
+        for j in range(side):
+            for l in range(lanes):
+                v = stage[l, pl.ds(i * pitch + j, slots, stride=side * pitch), :]
+                p[i + 1, j + 1, :, l * 128:(l + 1) * 128] = v.astype(BF16)
+        return 0
+    lax.fori_loop(0, side, take_row, 0)
+
+    pl.semaphore_wait(bar, total - 1)
+    def cot_copy(k):
+        d = lax.rem(b + k, nb)
+        return pltpu.make_async_remote_copy(
+            src_ref=cin.at[d], dst_ref=cgot.at[b], send_sem=cs.at[k], recv_sem=cr.at[k],
+            device_id=(d, t), device_id_type=MESH_ID)
+    lax.fori_loop(1, nb, lambda k, _: (cot_copy(k).start(), 0)[1], 0)
+
+    cw_load.wait()
+    turn = place.at[0] * 2 < place.dims[0]
+    flags = (lax.broadcasted_iota(jnp.int32, (slots, padded - per), 0) < live_ref[0]).astype(F32).astype(BF16)
+    m_rows = side * slots
+    def conv_row(k):
+        y = jnp.where(turn, side - 1 - k, k)
+        window = jnp.concatenate([p[y + a, c:c + side].reshape(m_rows, chan) for a in range(3) for c in range(3)], axis=1)
+        for u in range(towers):
+            pre = jnp.dot(window, cw[u], preferred_element_type=F32) + cbias_ref[u][None]
+            value, inc = gelu_pair(pre)
+            act[lax.rem(k, 3), :, :, u * cout:(u + 1) * cout] = value.reshape(side, slots, cout)
+            slope[y, :, :, u * cout:(u + 1) * cout] = inc.astype(slope.dtype).reshape(side, slots, cout)
+    def feature_copy(d):
+        return pltpu.make_async_remote_copy(
+            src_ref=feat.at[d], dst_ref=fin.at[me], send_sem=fs.at[d], recv_sem=fr.at[me],
+            device_id=device(d), device_id_type=MESH_ID)
+    def feature_wait(d):
+        return pltpu.make_async_remote_copy(
+            src_ref=feat.at[d], dst_ref=fin.at[d], send_sem=fs.at[d], recv_sem=fr.at[d],
+            device_id=device(d), device_id_type=MESH_ID)
+    pairs = nb // 2
+    conv_row(0)
+    def pooled_row(n, _):
+        lax.fori_loop(2 * n + 1, 2 * n + 3, lambda k, _: (conv_row(k), 0)[1], 0)
+        i = jnp.where(turn, pool - 1 - n, n)
+        s3 = act[0] + act[1] + act[2]
+        for j in range(pool):
+            p9 = (s3[2 * j] + s3[2 * j + 1] + s3[2 * j + 2]) * (1.0 / 9.0)
+            pooled[i * pool + j] = p9
+            at = pl.ds(pl.multiple_of((i * pool + j) * cout, cout), cout)
+            for u in range(towers):
+                m = cmix_ref[u, 0][None] * p9[:, :cout] + cmix_ref[u, 1][None] * p9[:, cout:]
+                fbuf[u, :, at] = m.astype(BF16)
+        def pair(q, _):
+            c = jnp.where(turn, pairs - 1 - q, q)
+            for u in range(towers):
+                v = fbuf[u, :, pl.ds(pl.multiple_of(c * 2 * per, 128), 2 * per)]
+                for h in range(2):
+                    d = (2 * c + h) * 2 + u
+                    feat[d, :, :per] = v[:, h * per:(h + 1) * per]
+                    feat[d, :, per:] = flags
+                    @pl.when(d != me)
+                    def _():
+                        feature_copy(d).start()
+            return 0
+        lax.fori_loop(n * pairs // pool, (n + 1) * pairs // pool, pair, 0)
+        return 0
+    lax.fori_loop(0, pool, pooled_row, 0)
+    fin[me] = feat[me]
+    def others(body):
+        lax.fori_loop(1, total, lambda k, _: (body(lax.rem(me + k, total)), 0)[1], 0)
+    others(lambda d: feature_wait(d).wait_recv())
+
+    got = fin[...].reshape(rows, padded)
+    flag = got[:, per:per + 1]
+    lower = (lax.broadcasted_iota(jnp.int32, (rows, rows), 1) < lax.broadcasted_iota(jnp.int32, (rows, rows), 0)).astype(BF16)
+    index = jnp.dot(lower, jnp.broadcast_to(flag, (rows, 128)), preferred_element_type=F32)[:, :1].astype(jnp.int32)
+    hit = (index == lax.broadcasted_iota(jnp.int32, (rows, live), 1)) & (flag.astype(F32) > 0.5)
+    spread[...] = hit.astype(F32).astype(BF16)
+    pack = lambda v: lax.dot_general(spread[...], v, (((0,), (0,)), ((), ())), preferred_element_type=F32)
+    f_ref[...] = pack(got[:, :per]).astype(BF16)
+    for c in w_loads:
+        c.wait()
+    chips = [((k // (place.dims[1] * place.dims[2])), (k // place.dims[2]) % place.dims[1], k % place.dims[2]) for k in range(nb)]
+    for k, i in enumerate(chips):
+        s[i] = jnp.dot(f_ref[...], w[k], preferred_element_type=F32).astype(BF16)
+    size = live // (2 * parts)
+    pieces = []
+    for n in range(2 * parts):
+        half = n % 2
+        low = pl.ds(((n // 2) + half * parts) * size, size)
+        pieces.append((Sum(place, 2 - half, s.at[:, :, :, low], r1.at[n], t1.at[n], r2.at[n], t2.at[n], r3.at[n],
+                           g.at[:, :, :, low], gs.at[n], gr.at[n]), low))
+    for piece, _ in pieces:
+        piece.send1()
+    lax.fori_loop(1, nb, lambda k, _: (cot_copy(k).wait_recv(), 0)[1], 0)
+    cots[0] = pack(cgot[...].reshape(rows, cols)).astype(BF16)
+    cot_swap = send(cots.at[0], cots.at[1], xs.at[0], xr.at[0], other)
+    mine_cols = pl.ds(pl.multiple_of(b * cols, 128), cols)
+    mixes = lambda i, j: fmix_ref[i, j:j + 1, mine_cols]
+    first = t == 0
+    own = jnp.where(first, mixes(0, 0), mixes(1, 1))
+    cross = jnp.where(first, mixes(0, 1), mixes(1, 0))
+    back = jnp.where(first, mixes(1, 0), mixes(0, 1))
+    here = place.at
+    def gate_piece(piece, low):
+        value, inc = gelu_pair(piece.result() + bias_ref[:, mine_cols])
+        gates[0, low, :] = value.astype(BF16)
+        d_gate = own * cots[0, low, :].astype(F32) + back * cots[1, low, :].astype(F32)
+        g[here[0], here[1], here[2], low, :] = (d_gate * inc).astype(BF16)
+        piece.gather1()
+    todo = [lambda q, low: q.send2(), lambda q, low: q.send3(), gate_piece]
+    for step in range(parts + 2):
+        for k in range(3):
+            c = step - k
+            if 0 <= c < parts:
+                if k == 2 and c == 0:
+                    cot_swap.wait_recv()
+                for piece, low in pieces[2 * c:2 * c + 2]:
+                    todo[k](piece, low)
+    gate_swap = send(gates.at[0], gates.at[1], xs.at[1], xr.at[1], other)
+    for piece, low in pieces[:2]:
+        piece.gather2()
+    gate_swap.wait_recv()
+    gate, cot, gate_other = gates[0].astype(F32), cots[0].astype(F32), gates[1].astype(F32)
+    total_rows = [jnp.sum(cot * gate, axis=0, keepdims=True), jnp.sum(cot * gate_other, axis=0, keepdims=True),
+                  jnp.sum(g[here[0], here[1], here[2]].astype(F32), axis=0, keepdims=True)]
+    wide[me] = jnp.concatenate(total_rows + [jnp.zeros((5, cols), F32)], axis=0)
+    def sums_copy(k):
+        d = lax.rem(me + k, total)
+        return pltpu.make_async_remote_copy(
+            src_ref=wide.at[me], dst_ref=wide.at[me], send_sem=ms.at[k], recv_sem=mr.at[k],
+            device_id=device(d), device_id_type=MESH_ID)
+    def drain(k, _):
+        cot_copy(k).wait_send()
+        return 0
+    lax.fori_loop(1, nb, drain, 0)
+    stitched = (own * gate + cross * gate_other).astype(BF16)
+    cin[...] = jnp.dot(spread[...], stitched, preferred_element_type=F32).astype(BF16).reshape(cin.shape)
+    def stitched_copy(k):
+        d = lax.rem(b + k, nb)
+        return pltpu.make_async_remote_copy(
+            src_ref=cin.at[d], dst_ref=sgot.at[b], send_sem=ss.at[k], recv_sem=sr.at[k],
+            device_id=(d, t), device_id_type=MESH_ID)
+    lax.fori_loop(1, total, lambda k, _: (sums_copy(k).start(), 0)[1], 0)
+    lax.fori_loop(1, nb, lambda k, _: (stitched_copy(k).start(), 0)[1], 0)
+    sgot[b] = cin[b]
+    for c in range(1, parts):
+        for piece, low in pieces[2 * c:2 * c + 2]:
+            piece.gather2()
+        for piece, low in pieces[2 * c - 2:2 * c]:
+            piece.gather3()
+    for piece, low in pieces[-2:]:
+        piece.gather3()
+    for piece, low in pieces:
+        piece.arrive()
+    acc[...] = jnp.zeros(acc.shape, F32)
+    for k, i in enumerate(chips):
+        acc[...] += lax.dot_general(g[i], w[k], (((1,), (1,)), ((), ())), preferred_element_type=F32)
+    others(lambda d: feature_wait(d).wait_send())
+    feat[:, :, :per] = jnp.dot(spread[...], acc[...].astype(BF16), preferred_element_type=F32).astype(BF16).reshape(total, slots, per)
+    def grad_copy(k):
+        d = lax.rem(me + k, total)
+        return pltpu.make_async_remote_copy(
+            src_ref=feat.at[d], dst_ref=dm.at[t, b], send_sem=ds.at[k], recv_sem=dr.at[k],
+            device_id=device(d), device_id_type=MESH_ID)
+    lax.fori_loop(1, total, lambda k, _: (grad_copy(k).start(), 0)[1], 0)
+    dm[t, b] = feat[me]
+    lax.fori_loop(1, nb, lambda k, _: (stitched_copy(k).wait_recv(), 0)[1], 0)
+    for k in range(nb):
+        out_ref[0, :, k * cols:(k + 1) * cols] = sgot[k]
+    lax.fori_loop(1, total, lambda k, _: (sums_copy(k).wait_recv(), 0)[1], 0)
+    for k in range(nb):
+        at = slice(k * cols, (k + 1) * cols)
+        for u in range(2):
+            stitch_ref[u, u:u + 1, at] = wide[2 * k + u, 0:1]
+            stitch_ref[u, 1 - u:2 - u, at] = wide[2 * k + u, 1:2]
+            fbias_ref[u:u + 1, at] = wide[2 * k + u, 2:3]
+    lax.fori_loop(1, total, lambda k, _: (grad_copy(k).wait_recv(), 0)[1], 0)
+
+    for u in range(towers):
+        for k in range(nb):
+            fbuf[u, :, k * per:(k + 1) * per] = dm[u, k, :, :per]
+    z[0] = jnp.zeros(z.shape[1:], F32)
+    z[pool + 1] = jnp.zeros(z.shape[1:], F32)
+    mixed = [[jnp.zeros((slots, cout), F32)] * 2 for _ in range(2)]
+    for i in range(pool):
+        z[i + 1, 0] = jnp.zeros(z.shape[2:], F32)
+        z[i + 1, pool + 1] = jnp.zeros(z.shape[2:], F32)
+        for j in range(pool):
+            q = i * pool + j
+            dmx = [fbuf[u, :, q * cout:(q + 1) * cout].astype(F32) for u in range(towers)]
+            for u in range(towers):
+                pu = pooled[q, :, u * cout:(u + 1) * cout]
+                for v in range(towers):
+                    mixed[v][u] = mixed[v][u] + dmx[v] * pu
+                z[i + 1, j + 1, :, u * cout:(u + 1) * cout] = (cmix_ref[0, u][None] * dmx[0] + cmix_ref[1, u][None] * dmx[1]) * (1.0 / 9.0)
+    lines = [jnp.concatenate([jnp.sum(mixed[v][u], axis=0, keepdims=True) for u in range(2)], axis=1) for v in range(2)]
+    sums_t[...] = jnp.concatenate([jnp.zeros((1, wide_c), F32)] + lines + [jnp.zeros((125, wide_c), F32)], axis=0).T
+    cells = side * side
+    dpad[0] = jnp.zeros(dpad.shape[1:], BF16)
+    dpad[side + 1] = jnp.zeros(dpad.shape[1:], BF16)
+    d2[cells:] = jnp.zeros((d2.shape[0] - cells, slots, wide_c), BF16)
+    def drow(y, src):
+        dpad[y + 1, 0] = jnp.zeros((slots, wide_c), BF16)
+        dpad[y + 1, side + 1] = jnp.zeros((slots, wide_c), BF16)
+        for x in range(side):
+            j = x // 2
+            v = src(j + 1) if x % 2 else src(j) + src(j + 1)
+            d = (v * slope[y, x].astype(F32)).astype(BF16)
+            dpad[y + 1, x + 1] = d
+            d2[y * side + x] = d
+    def two(i, _):
+        drow(2 * i, lambda j: z[i, j] + z[i + 1, j])
+        drow(2 * i + 1, lambda j: z[i + 1, j])
+        return 0
+    lax.fori_loop(0, pool, two, 0)
+    drow(side - 1, lambda j: z[pool, j] + z[pool + 1, j])
+    block = 256 // slots
+    def flip(k, _):
+        dt[:, pl.ds(pl.multiple_of(k * 256, 256), 256)] = d2[pl.ds(k * block, block)].reshape(256, wide_c).T
+        return 0
+    lax.fori_loop(0, d2.shape[0] // block, flip, 0)
+
+    chunks, span = grad_ref.shape[1], grad_ref.shape[-1]
+    tail = dt.shape[1] - cells * slots
+    give = w.at[0:chunks, 0:cout]
+    take = w.at[0:chunks, cout:2 * cout]
+
+    def window(n):
+        parts_ = []
+        low = n * span
+        while low < (n + 1) * span:
+            k = low // chan
+            if k < 9:
+                high = min((n + 1) * span, (k + 1) * chan)
+                a, c = k // 3, k % 3
+                parts_.append(p[a:a + side, c:c + side, :, low - k * chan:high - k * chan].reshape(cells * slots, high - low))
+                low = high
+            else:
+                parts_.append(jnp.ones((cells * slots, (n + 1) * span - low), BF16))
+                low = (n + 1) * span
+        win = parts_[0] if len(parts_) == 1 else jnp.concatenate(parts_, axis=1)
+        return jnp.concatenate([win, jnp.zeros((tail, span), BF16)], axis=0)
+
+    lots = [Sum(place, 2 - n % 2, cs_.at[n], cr1.at[n], ct1.at[n], cr2.at[n], ct2.at[n], cr3.at[n], grad_ref.at[t, n], ks.at[n], kr.at[n])
+            for n in range(chunks)]
+    core, share_back = {}, {}
+
+    def compute(n):
+        win = window(n)
+        def half(u):
+            at = pl.ds(pl.multiple_of(u * cout, cout), cout)
+            v = jnp.dot(dt[at, :], win, preferred_element_type=F32)
+            if n == chunks - 1:
+                extra = sums_t[at, :]
+                lane = lax.broadcasted_iota(jnp.int32, extra.shape, 1)
+                v = jnp.concatenate([v[:, :span - 128], jnp.where(lane == 0, v[:, span - 128:], extra)], axis=1)
+            return v
+        give[n] = half(1 - t).astype(BF16)
+        core[n] = send(give.at[n], take.at[n], hs.at[n, 0], hr.at[n, 0], other)
+        keep[n % keep.shape[0]] = half(t)
+
+    def merge(n):
+        core[n].wait_recv()
+        cs_[n] = (keep[n % keep.shape[0]] + take[n].astype(F32)).astype(BF16).reshape(cs_.shape[1:])
+        lots[n].send1()
+
+    def finish(n):
+        grad_ref[t, n, here[0], here[1], here[2]] = lots[n].result().astype(BF16)
+        lots[n].gather1()
+
+    def share(n):
+        lots[n].arrive()
+        share_back[n] = send(grad_ref.at[t, n], grad_ref.at[t, n], hs.at[n, 1], hr.at[n, 1], other)
+
+    def xrow(y):
+        lhs = jnp.concatenate([dpad[y + 2 - a, 2 - c:2 - c + side, :, u * cout:(u + 1) * cout].reshape(m_rows, cout)
+                               for u in range(towers) for a in range(3) for c in range(3)], axis=1)
+        rhs = jnp.concatenate([cw[u, (a * 3 + c) * chan:(a * 3 + c + 1) * chan, :]
+                               for u in range(towers) for a in range(3) for c in range(3)], axis=1)
+        o = lax.dot_general(lhs, rhs, (((1,), (1,)), ((), ())), preferred_element_type=F32).reshape(side, slots, chan)
+        for x in range(side):
+            for l in range(lanes):
+                stage[l, pl.ds(y * pitch + x, slots, stride=side * pitch), :] = o[x, :, l * 128:(l + 1) * 128]
+
+    stores = []
+    def flush(q):
+        def put(k, _):
+            xin[k // side, k % side] = jnp.concatenate(
+                [stage[l, pl.ds(pl.multiple_of(k * pitch, pitch), side), :] for l in range(lanes)], axis=1).astype(BF16)
+            return 0
+        lax.fori_loop(q * crops * side, (q + 1) * crops * side, put, 0, unroll=4)
+        c = pltpu.make_async_copy(xin.at[pl.ds(q * crops, crops)], dx_hbm.at[pl.ds(q * crops, crops)], xsem.at[q])
+        c.start()
+        stores.append(c)
+
+    side_work = [functools.partial(xrow, y) for y in range(side)] + [functools.partial(flush, q) for q in range(groups)]
+    work = [merge, lambda n: lots[n].send2(), lambda n: lots[n].send3(), finish,
+            lambda n: lots[n].gather2(), lambda n: lots[n].gather3(), share, lambda n: share_back[n].wait_recv()]
+    for step in range(chunks + 3 * (len(work) - 1) + 1):
+        if step < chunks:
+            compute(step)
+        if step >= 14 and side_work:
+            side_work.pop(0)()
+        for k, job in enumerate(work):
+            n = step - 1 - 3 * k
+            if 0 <= n < chunks:
+                job(n)
+    for job in side_work:
+        job()
+    for c in stores:
+        c.wait()
+    for piece, _ in pieces:
+        piece.close()
+    cot_swap.wait_send()
+    gate_swap.wait_send()
+    for n in range(chunks):
+        lots[n].close()
+        core[n].wait_send()
+        share_back[n].wait_send()
+    def drain_all(k, _):
+        grad_copy(k).wait_send()
+        sums_copy(k).wait_send()
+        return 0
+    lax.fori_loop(1, total, drain_all, 0)
+    lax.fori_loop(1, nb, lambda k, _: (stitched_copy(k).wait_send(), 0)[1], 0)
+
+
+def whole_layer(live_rows, x, cw, cbias, cmix, cot, w, fbias, fmix, nb, parts=2):
+    slots, side, _, chan = x.shape
+    towers, _, cout = cw.shape
+    per, fc = w.shape
+    cols = fc // nb
+    total = 2 * nb
+    rows = total * slots
+    live = rows // 2
+    pool = (side - 3) // 2 + 1
+    padded = per // 128 * 128 + 128
+    wide = towers * cout
+    d0, d1, d2 = torus(nb)
+    size = live // (2 * parts)
+    n = 2 * parts
+    span = 256
+    chunks = (9 * chan + 128) // span
+    h = cout // nb
+    cells = -(-side * side * slots // 256) * 256 // slots
+    V = pl.BlockSpec(memory_space=pltpu.VMEM)
+    A = pl.BlockSpec(memory_space=pl.ANY)
+    vm = lambda *shape: pltpu.VMEM(shape, BF16)
+    vf = lambda *shape: pltpu.VMEM(shape, F32)
+    dma = lambda *shape: pltpu.SemaphoreType.DMA(shape)
+    shape = jax.ShapeDtypeStruct
+    return pl.pallas_call(
+        functools.partial(whole_kernel, parts, per),
+        out_shape=[shape((1, 2 * slots, fc), BF16), shape(x.shape, BF16), shape((live, per), BF16),
+                   shape((d0, d1, d2, live, cols), BF16), shape((towers, chunks, d0, d1, d2, h, span), BF16),
+                   shape((2, 2, fc), F32), shape((2, fc), F32)],
+        in_specs=[pl.BlockSpec(memory_space=pltpu.SMEM), A, A, V, V, V, A, V, V],
+        out_specs=[V, A, V, V, V, V, V],
+        scratch_shapes=[
+            vm(*x.shape), vm(*cw.shape), vf(chan // 128, slots * side * 16, 128), vf(3, side, slots, wide),
+            vm(side + 2, side + 2, slots, chan), vm(side, side, slots, wide), vf(pool * pool, slots, wide),
+            vm(towers, slots, nb * per), vm(total, slots, padded), vm(total, slots, padded), vm(towers, nb, slots, padded),
+            vm(nb, per, cols), vm(nb, 2 * slots, cols), vm(nb, 2 * slots, cols), vm(nb, 2 * slots, cols), vm(rows, live),
+            vm(d0, d1, d2, live, cols), vm(n, d1 - 1, d0, d1, size, cols), vm(n, d0, d1, size, cols),
+            vm(n, d1 - 1, d0, size, cols), vm(n, d0, size, cols), vm(n, d0 - 1, size, cols),
+            vm(2, live, cols), vm(2, live, cols), vf(total, 8, cols), vf(live, per),
+            vf(pool + 2, pool + 2, slots, wide), vm(side + 2, side + 2, slots, wide), vm(cells, slots, wide), vm(wide, cells * slots),
+            vf(2, cout, span), vm(chunks, d0, d1, d2, h, span), vm(chunks, d1 - 1, d0, d1, h, span), vm(chunks, d0, d1, h, span),
+            vm(chunks, d1 - 1, d0, h, span), vm(chunks, d0, h, span), vm(chunks, d0 - 1, h, span), vf(wide, 128),
+            dma(4), pltpu.SemaphoreType.DMA, dma(nb), dma(total), dma(total), dma(nb), dma(nb), dma(2), dma(2), dma(nb), dma(nb),
+            dma(total), dma(total), dma(n, hops(nb)), dma(n, hops(nb)), dma(total), dma(total),
+            dma(chunks, hops(nb)), dma(chunks, hops(nb)), dma(chunks, 2), dma(chunks, 2)],
+        compiler_params=pltpu.CompilerParams(collective_id=1, has_side_effects=True, vmem_limit_bytes=63 * 2**20),
+    )(live_rows, x, cw, cbias, cmix, cot, w, fbias, fmix)
+
+
+def write_kernel(f_ref, g_ref, dw_ref, fc_ref, conv_ref, bias_ref, mix_ref):
+    fc_ref[0] = lax.dot_general(f_ref[...], g_ref[0], (((0,), (0,)), ((), ())), preferred_element_type=F32)
+    flat = [dw_ref[u, 0].astype(F32).T for u in range(dw_ref.shape[0])]
+    half = dw_ref.shape[-1] - 128
+    for u, v in enumerate(flat):
+        conv_ref[u] = v
+        bias_ref[u:u + 1] = v[half:half + 1]
+        mix_ref[0, u:u + 1] = v[half + 1:half + 2]
+        mix_ref[1, u:u + 1] = v[half + 2:half + 3]
+
+
+def write_grads(f, g, dw, nb, cols, ktaps):
+    live, per = f.shape
+    towers, chunks, cout, span = dw.shape
+    last = chunks - 1
+    shape = jax.ShapeDtypeStruct
+    return pl.pallas_call(
+        write_kernel,
+        grid=(nb,),
+        out_shape=[shape((1, per, nb * cols), F32), shape((towers, ktaps, cout), F32), shape((towers, cout), F32), shape((2, towers, cout), F32)],
+        in_specs=[pl.BlockSpec((live, per), lambda k: (0, 0)), pl.BlockSpec((1, live, cols), lambda k: (k, 0, 0)),
+                  pl.BlockSpec((towers, 1, cout, span), lambda k: (0, jnp.minimum(k, last), 0, 0))],
+        out_specs=[pl.BlockSpec((1, per, cols), lambda k: (0, 0, k)),
+                   pl.BlockSpec((towers, span, cout), lambda k: (0, jnp.minimum(k, last), 0)),
+                   pl.BlockSpec((towers, cout), lambda k: (0, 0)), pl.BlockSpec((2, towers, cout), lambda k: (0, 0, 0))],
+        compiler_params=pltpu.CompilerParams(vmem_limit_bytes=32 * 2**20),
+    )(f, g, dw)
+
+
+def shards(crop_pixels, live_rows, conv_weight, conv_bias, stitch_conv, fc_weight, fc_bias, stitch_fc, cotangent):
+    slots = crop_pixels.shape[0]
+    nb = lax.axis_size("batch")
+    fc = fc_weight.shape[2]
+    cols = fc // nb
+    cin, cout = conv_weight.shape[3:]
+    live = slots * nb
+    stitched, dx, f, dh, dw, d_stitch_fc, d_fc_bias = whole_layer(
+        live_rows, crop_pixels, conv_weight.reshape(2, 9 * cin, cout), conv_bias, stitch_conv, cotangent[0], fc_weight[0], fc_bias, stitch_fc, nb)
+    dw = dw.reshape(2, dw.shape[1], cout, dw.shape[-1])
+    d_fc_weight, d_kernel, d_conv_bias, d_stitch_conv = write_grads(f, dh.reshape(nb, live, cols), dw, nb, cols, 9 * cin)
+    return stitched, dx, d_kernel.reshape(conv_weight.shape), d_conv_bias, d_stitch_conv, d_fc_weight, d_fc_bias, d_stitch_fc
 
 
 def solution(mesh):
@@ -254,4 +830,5 @@
         P("tower", "batch", None), P(("batch", "tower"), None, None, None), P(), P(), P(),
         P("tower", "batch", None), P(), P(),
     )
-    return jax.shard_map(shards, mesh=mesh, in_specs=in_specs, out_specs=out_specs, check_vma=False)
+    body = shards if mesh.shape["batch"] == 16 else plain_shards
+    return jax.shard_map(body, mesh=mesh, in_specs=in_specs, out_specs=out_specs, check_vma=False)

time: 581 us -> 199 us (0.34)
  waiting for transfers between devices: 265 us -> 0 us
  Pallas kernels: 65.5 us -> 186 us
  blocking collectives: 108 us -> 0 us
  other arithmetic: 43.3 us -> 0 us
  local copies, waits for them, and re-layouts: 43.5 us -> 10.9 us
  starting transfers between devices: 20.7 us -> 0 us
  matrix products: 18.1 us -> 0 us
  between operations: 14.6 us -> 1.31 us
    pallas_call x2, Pallas kernels: 65.5 us -> 186 us  [the longest x1 176 us: whole_layer(): pl.pallas_call(functools.partial(whole_kernel, parts, per), out_shape=[sh...]
    psum x1 -> x0, waiting for transfers between devices: 112 us -> none  [shards(): dw = lax.psum(dw, both)]
    reduce_scatter x1 -> x0, waiting for transfers between devices: 73.7 us -> none  [shards(): hidden = lax.psum_scatter(part, 'batch', scatter_dimension=1, tiled=True)]
    all_gather x1 -> x0, waiting for transfers between devices: 65.4 us -> none  [shards(): dh = lax.all_gather(dh, 'batch', axis=1, tiled=True)]
    all_gather x1 -> x0, blocking collectives: 46 us -> none  [shards(): lax.all_gather(sums, both, axis=0).reshape(nb, 2, 3, cols)]
    unnamed x1 -> x0, blocking collectives: 39.6 us -> none
    select_n x2 -> x0, other arithmetic: 31.8 us -> none  [the longest x1 31 us: shards(): jnp.where(slot % slots < counts[slot // slots], start[slot // slots] + sl...]
    all_to_all x1 -> x0, blocking collectives: 22.2 us -> none  [shards(): dm = lax.all_to_all(expand(df).reshape(2 * nb, slots, per), both, 0, 0)]
  transfers between devices with their start and end apart: 8 -> 0, of which waited for: 6 -> 0; matrix products, arithmetic and copies ran while one was open for 10% -> 0% of each run, Pallas kernels for 0% -> 0%
where the time goes in v4:
time: 199 us
  Pallas kernels  186 us (93%)
  local copies, waits for them, and re-layouts  10.9 us (5%)
    pallas_call x1, Pallas kernels, whole_layer(): pl.pallas_call(functools.partial(whole_kernel, parts, per), out_shape=[sh...  176 us
    unnamed x17, local copies, waits for them, and re-layouts  10.9 us
    pallas_call x1, Pallas kernels, write_grads(): pl.pallas_call(write_kernel, grid=(nb,), out_shape=[shape((1, per, nb * c...  10.5 us

profile of v4, /device:TPU:1, one launch (start us, length us, event | category | flops | bytes accessed | tf_op | source)
XLA Modules:
  0.0 198.5 jit_solution(17215132426393688375)
XLA Ops:
  1.3 3.6 %copy.17.x_hbm = bf16[16,13,13,384]{3,2,1,0:T(8,128)(2,1)} copy(bf16[16,13,13,384]{3,0,2,1:T(8,128)(2,1)} %param.9) | data formatting | bytes 4153344 | tf_op args[0]
  4.9 175.9 %shard_map.152 = (bf16[1,32,4096]{2,1,0:T(8,128)(2,1)}, bf16[16,13,13,384]{3,2,1,0:T(8,128)(2,1)}, bf16[256,576]{1,0:T(8,128)(2,1)}, bf16[4,2,2,256,256]{4,3,2,1...) custom-call(s32[1]{0:T(128)S(6)} %copy.22.live_ref, ...), custom_call_target="tpu_custom_call" | custom-call | tf_op jit(solution)/shard_map/pallas_call | solution.py:756
  180.8 0.0 copy-start
  180.8 0.0 copy-start.2
  180.8 3.7 %copy.18 = bf16[16,13,13,384]{3,0,2,1:T(8,128)(2,1)} copy(bf16[16,13,13,384]{3,2,1,0:T(8,128)(2,1)} %get-tuple-element.31) | data formatting | bytes 4153344
  184.5 0.0 copy-done
  184.5 0.0 copy-done.2
  184.5 0.0 copy-start.1
  184.5 1.6 copy-done.1
  186.1 0.0 copy-start.3
  186.1 0.0 copy-start.5
  186.1 0.0 copy-start.4
  186.1 10.5 %shard_map.153 = (f32[1,576,4096]{2,1,0:T(8,128)}, f32[2,3456,256]{2,1,0:T(8,128)}, f32[2,256]{1,0:T(2,128)}, f32[2,2,256]{2,1,0:T(2,128)}) custom-call(bf16[256,576]{1,0:T(8,128)(2,1)S(1)} %copy-done.2, bf16[16,256,256]{2,1,0:T(8,128)(2,1)S(1)} %bitcast.7, bf16[2,14,256,256]{3,2,1,0:T(8,128)(2,1)S(1)} %bitcast.6), custom_call_target="tpu_custom_call" | custom-call | tf_op jit(solution)/shard_map/pallas_call | solution.py:797
  196.6 0.0 copy-done.3
  196.6 0.7 copy.23
  197.3 0.0 copy-done.5
  197.3 0.6 copy.24
  197.9 0.0 copy-done.4
  197.9 0.6 copy.25
Async XLA Ops:
  180.8 3.7 %copy-start = (bf16[2,14,4,2,2,16,256]{6,5,4,3,2,1,0:T(8,128)(2,1)S(1)}, bf16[2,14,4,2,2,16,256]{6,5,4,3,2,1,0:T(8,128)(2,1)}, u32[]{:S(2)}) copy-start(bf16[2,14,4,2,2,16,256]{6,5,4,3,2,1,0:T(8,128)(2,1)} %get-tuple-element.23) | copy-start | bytes 11010052
  180.8 3.7 %copy-start.2 = (bf16[256,576]{1,0:T(8,128)(2,1)S(1)}, bf16[256,576]{1,0:T(8,128)(2,1)}, u32[]{:S(2)}) copy-start(bf16[256,576]{1,0:T(8,128)(2,1)} %get-tuple-element.21.f_ref) | copy-start | bytes 884740
  184.5 1.6 copy-start.1
  186.1 10.5 %copy-start.3 = (bf16[1,32,4096]{2,1,0:T(8,128)(2,1)S(1)}, bf16[1,32,4096]{2,1,0:T(8,128)(2,1)}, u32[]{:S(2)}) copy-start(bf16[1,32,4096]{2,1,0:T(8,128)(2,1)} %get-tuple-element.46) | copy-start | bytes 786436
  186.1 11.2 %copy-start.5 = (f32[2,4096]{1,0:T(2,128)S(1)}, f32[2,4096]{1,0:T(2,128)}, u32[]{:S(2)}) copy-start(f32[2,4096]{1,0:T(2,128)} %get-tuple-element.52) | copy-start | bytes 98308
  186.1 11.8 %copy-start.4 = (f32[2,2,4096]{2,1,0:T(2,128)S(1)}, f32[2,2,4096]{2,1,0:T(2,128)}, u32[]{:S(2)}) copy-start(f32[2,2,4096]{2,1,0:T(2,128)} %get-tuple-element.53) | copy-start | bytes 196612

commit v5 on v4

--- a/solution.py
+++ b/solution.py
@@ -245,12 +245,12 @@
     rows = jnp.concatenate([jnp.concatenate([jnp.sum(acc[t][u], axis=0, keepdims=True) for u in range(2)], axis=1) for t in range(2)], axis=0)
     small_ref[:, 128:256] = jnp.concatenate([rows, jnp.zeros((126, wide), F32)], axis=0).T
     pitch = 16
-    def xrow(y):
-        lhs = jnp.concatenate([dpad[y + 2 - a, 2 - b:2 - b + side, :, t * cout:(t + 1) * cout].reshape(side * slots, cout)
+    def xrow(y, n=1):
+        lhs = jnp.concatenate([dpad[pl.ds(y + 2 - a, n), 2 - b:2 - b + side, :, t * cout:(t + 1) * cout].reshape(n * side * slots, cout)
                                for t in range(towers) for a in range(3) for b in range(3)], axis=1)
         rhs = jnp.concatenate([w_ref[t, (a * 3 + b) * cin:(a * 3 + b + 1) * cin, :]
                                for t in range(towers) for a in range(3) for b in range(3)], axis=1)
-        out = lax.dot_general(lhs, rhs, (((1,), (1,)), ((), ())), preferred_element_type=F32).reshape(side, slots, cin)
+        out = lax.dot_general(lhs, rhs, (((1,), (1,)), ((), ())), preferred_element_type=F32).reshape(n * side, slots, cin)
         for x in range(side):
             for l in range(cin // 128):
                 stage[l, pl.ds(y * pitch + x, slots, stride=side * pitch), :] = out[x, :, l * 128:(l + 1) * 128]
@@ -351,7 +351,7 @@
 
 def whole_kernel(parts, per, live_ref, x_hbm, cw_hbm, cbias_ref, cmix_ref, cot_ref, w_hbm, bias_ref, fmix_ref,
                  out_ref, dx_hbm, f_ref, g, grad_ref, stitch_ref, fbias_ref,
-                 xin, cw, stage, act, p, slope, pooled, fbuf, feat, fin, dm, w, cin, cgot, sgot, spread,
+                 dxv, cw, act, p, slope, pooled, fbuf, feat, fin, dm, w, cin, cgot, sgot, spread,
                  s, r1, t1, r2, t2, r3, gates, cots, wide, acc,
                  z, dpad, d2, dt, keep, cs_, cr1, ct1, cr2, ct2, cr3, sums_t,
                  xsem, lsem, wsem, fs, fr, cs, cr, xs, xr, ss, sr, ms, mr, gs, gr, ds, dr, ks, kr, hs, hr):
@@ -360,12 +360,10 @@
     b, t = place.b, place.t
     me = b * 2 + t
     total = 2 * nb
-    slots, side, _, chan = xin.shape
+    side, _, slots, chan = dxv.shape
     towers, _, cout = cw.shape
     pool = (side - 3) // 2 + 1
     wide_c = towers * cout
-    pitch = 16
-    lanes = chan // 128
     padded = feat.shape[2]
     rows = total * slots
     live = rows // 2
@@ -373,11 +371,8 @@
     other = (b, 1 - t)
     device = lambda d: (d // 2, d % 2)
 
-    groups = xsem.shape[0]
-    crops = slots // groups
-    loads = [pltpu.make_async_copy(x_hbm.at[pl.ds(k * crops, crops)], xin.at[pl.ds(k * crops, crops)], xsem.at[k]) for k in range(groups)]
-    for c in loads:
-        c.start()
+    load = pltpu.make_async_copy(x_hbm, p.at[pl.ds(1, side), pl.ds(1, side)], xsem.at[0])
+    load.start()
     cw_load = pltpu.make_async_copy(cw_hbm, cw, lsem)
     cw_load.start()
     w_loads = [pltpu.make_async_copy(w_hbm.at[:, pl.ds(k * cols, cols)], w.at[k], wsem.at[k]) for k in range(nb)]
@@ -394,23 +389,9 @@
 
     p[0] = jnp.zeros(p.shape[1:], BF16)
     p[side + 1] = jnp.zeros(p.shape[1:], BF16)
-    for q in range(groups):
-        loads[q].wait()
-        def put(k, _):
-            v = xin[k // side, k % side].astype(F32)
-            for l in range(lanes):
-                stage[l, pl.ds(pl.multiple_of(k * pitch, pitch), side), :] = v[:, l * 128:(l + 1) * 128]
-            return 0
-        lax.fori_loop(q * crops * side, (q + 1) * crops * side, put, 0, unroll=4)
-    def take_row(i, _):
+    for i in range(side):
         p[i + 1, 0] = jnp.zeros((slots, chan), BF16)
         p[i + 1, side + 1] = jnp.zeros((slots, chan), BF16)
-        for j in range(side):
-            for l in range(lanes):
-                v = stage[l, pl.ds(i * pitch + j, slots, stride=side * pitch), :]
-                p[i + 1, j + 1, :, l * 128:(l + 1) * 128] = v.astype(BF16)
-        return 0
-    lax.fori_loop(0, side, take_row, 0)
 
     pl.semaphore_wait(bar, total - 1)
     def cot_copy(k):
@@ -420,6 +401,7 @@
             device_id=(d, t), device_id_type=MESH_ID)
     lax.fori_loop(1, nb, lambda k, _: (cot_copy(k).start(), 0)[1], 0)
 
+    load.wait()
     cw_load.wait()
     turn = place.at[0] * 2 < place.dims[0]
     flags = (lax.broadcasted_iota(jnp.int32, (slots, padded - per), 0) < live_ref[0]).astype(F32).astype(BF16)
@@ -480,12 +462,12 @@
     hit = (index == lax.broadcasted_iota(jnp.int32, (rows, live), 1)) & (flag.astype(F32) > 0.5)
     spread[...] = hit.astype(F32).astype(BF16)
     pack = lambda v: lax.dot_general(spread[...], v, (((0,), (0,)), ((), ())), preferred_element_type=F32)
-    f_ref[...] = pack(got[:, :per]).astype(BF16)
+    f = pack(got[:, :per]).astype(BF16)
     for c in w_loads:
         c.wait()
     chips = [((k // (place.dims[1] * place.dims[2])), (k // place.dims[2]) % place.dims[1], k % place.dims[2]) for k in range(nb)]
     for k, i in enumerate(chips):
-        s[i] = jnp.dot(f_ref[...], w[k], preferred_element_type=F32).astype(BF16)
+        s[i] = jnp.dot(f, w[k], preferred_element_type=F32).astype(BF16)
     size = live // (2 * parts)
     pieces = []
     for n in range(2 * parts):
@@ -495,6 +477,7 @@
                            g.at[:, :, :, low], gs.at[n], gr.at[n]), low))
     for piece, _ in pieces:
         piece.send1()
+    f_ref[...] = f.T
     lax.fori_loop(1, nb, lambda k, _: (cot_copy(k).wait_recv(), 0)[1], 0)
     cots[0] = pack(cgot[...].reshape(rows, cols)).astype(BF16)
     cot_swap = send(cots.at[0], cots.at[1], xs.at[0], xr.at[0], other)
@@ -682,22 +665,13 @@
         rhs = jnp.concatenate([cw[u, (a * 3 + c) * chan:(a * 3 + c + 1) * chan, :]
                                for u in range(towers) for a in range(3) for c in range(3)], axis=1)
         o = lax.dot_general(lhs, rhs, (((1,), (1,)), ((), ())), preferred_element_type=F32).reshape(side, slots, chan)
-        for x in range(side):
-            for l in range(lanes):
-                stage[l, pl.ds(y * pitch + x, slots, stride=side * pitch), :] = o[x, :, l * 128:(l + 1) * 128]
-
-    stores = []
-    def flush(q):
-        def put(k, _):
-            xin[k // side, k % side] = jnp.concatenate(
-                [stage[l, pl.ds(pl.multiple_of(k * pitch, pitch), side), :] for l in range(lanes)], axis=1).astype(BF16)
-            return 0
-        lax.fori_loop(q * crops * side, (q + 1) * crops * side, put, 0, unroll=4)
-        c = pltpu.make_async_copy(xin.at[pl.ds(q * crops, crops)], dx_hbm.at[pl.ds(q * crops, crops)], xsem.at[q])
+        dxv[y] = o.astype(BF16)
+        c = pltpu.make_async_copy(dxv.at[y], dx_hbm.at[y], xsem.at[y])
         c.start()
         stores.append(c)
 
-    side_work = [functools.partial(xrow, y) for y in range(side)] + [functools.partial(flush, q) for q in range(groups)]
+    stores = []
+    side_work = [functools.partial(xrow, y) for y in range(side)]
     work = [merge, lambda n: lots[n].send2(), lambda n: lots[n].send3(), finish,
             lambda n: lots[n].gather2(), lambda n: lots[n].gather3(), share, lambda n: share_back[n].wait_recv()]
     for step in range(chunks + 3 * (len(work) - 1) + 1):
@@ -730,7 +704,7 @@
 
 
 def whole_layer(live_rows, x, cw, cbias, cmix, cot, w, fbias, fmix, nb, parts=2):
-    slots, side, _, chan = x.shape
+    side, _, slots, chan = x.shape
     towers, _, cout = cw.shape
     per, fc = w.shape
     cols = fc // nb
@@ -755,14 +729,14 @@
     shape = jax.ShapeDtypeStruct
     return pl.pallas_call(
         functools.partial(whole_kernel, parts, per),
-        out_shape=[shape((1, 2 * slots, fc), BF16), shape(x.shape, BF16), shape((live, per), BF16),
+        out_shape=[shape((1, 2 * slots, fc), BF16), shape(x.shape, BF16), shape((per, live), BF16),
                    shape((d0, d1, d2, live, cols), BF16), shape((towers, chunks, d0, d1, d2, h, span), BF16),
                    shape((2, 2, fc), F32), shape((2, fc), F32)],
         in_specs=[pl.BlockSpec(memory_space=pltpu.SMEM), A, A, V, V, V, A, V, V],
         out_specs=[V, A, V, V, V, V, V],
         scratch_shapes=[
-            vm(*x.shape), vm(*cw.shape), vf(chan // 128, slots * side * 16, 128), vf(3, side, slots, wide),
-            vm(side + 2, side + 2, slots, chan), vm(side, side, slots, wide), vf(pool * pool, slots, wide),
+            vm(*x.shape), vm(*cw.shape), vf(3, side, slots, wide),
+            vm(side + 2, side + 2, slots, chan), vf(side, side, slots, wide), vf(pool * pool, slots, wide),
             vm(towers, slots, nb * per), vm(total, slots, padded), vm(total, slots, padded), vm(towers, nb, slots, padded),
             vm(nb, per, cols), vm(nb, 2 * slots, cols), vm(nb, 2 * slots, cols), vm(nb, 2 * slots, cols), vm(rows, live),
             vm(d0, d1, d2, live, cols), vm(n, d1 - 1, d0, d1, size, cols), vm(n, d0, d1, size, cols),
@@ -771,40 +745,50 @@
             vf(pool + 2, pool + 2, slots, wide), vm(side + 2, side + 2, slots, wide), vm(cells, slots, wide), vm(wide, cells * slots),
             vf(2, cout, span), vm(chunks, d0, d1, d2, h, span), vm(chunks, d1 - 1, d0, d1, h, span), vm(chunks, d0, d1, h, span),
             vm(chunks, d1 - 1, d0, h, span), vm(chunks, d0, h, span), vm(chunks, d0 - 1, h, span), vf(wide, 128),
-            dma(4), pltpu.SemaphoreType.DMA, dma(nb), dma(total), dma(total), dma(nb), dma(nb), dma(2), dma(2), dma(nb), dma(nb),
+            dma(side), pltpu.SemaphoreType.DMA, dma(nb), dma(total), dma(total), dma(nb), dma(nb), dma(2), dma(2), dma(nb), dma(nb),
             dma(total), dma(total), dma(n, hops(nb)), dma(n, hops(nb)), dma(total), dma(total),
             dma(chunks, hops(nb)), dma(chunks, hops(nb)), dma(chunks, 2), dma(chunks, 2)],
         compiler_params=pltpu.CompilerParams(collective_id=1, has_side_effects=True, vmem_limit_bytes=63 * 2**20),
     )(live_rows, x, cw, cbias, cmix, cot, w, fbias, fmix)
 
 
-def write_kernel(f_ref, g_ref, dw_ref, fc_ref, conv_ref, bias_ref, mix_ref):
-    fc_ref[0] = lax.dot_general(f_ref[...], g_ref[0], (((0,), (0,)), ((), ())), preferred_element_type=F32)
-    flat = [dw_ref[u, 0].astype(F32).T for u in range(dw_ref.shape[0])]
-    half = dw_ref.shape[-1] - 128
+def write_kernel(f_ref, g_ref, dw_ref, st_ref, fs_ref, fb_ref, fc_ref, conv_ref, bias_ref, mix_ref, st_out, fs_out, fb_out):
+    cols = g_ref.shape[2]
+    for i in range(g_ref.shape[0]):
+        fc_ref[0, :, i * cols:(i + 1) * cols] = jnp.dot(f_ref[...], g_ref[i], preferred_element_type=F32)
+    flat = [jnp.concatenate([dw_ref[u, k].T for k in range(dw_ref.shape[1])], axis=0).astype(F32) for u in range(dw_ref.shape[0])]
+    half = flat[0].shape[0] - 128
     for u, v in enumerate(flat):
         conv_ref[u] = v
         bias_ref[u:u + 1] = v[half:half + 1]
         mix_ref[0, u:u + 1] = v[half + 1:half + 2]
         mix_ref[1, u:u + 1] = v[half + 2:half + 3]
-
-
-def write_grads(f, g, dw, nb, cols, ktaps):
-    live, per = f.shape
+    st_out[...] = st_ref[...]
+    fs_out[...] = fs_ref[...]
+    fb_out[...] = fb_ref[...]
+
+
+def write_grads(f, g, dw, stitched, d_stitch, d_bias, nb, cols, ktaps):
+    per, live = f.shape
     towers, chunks, cout, span = dw.shape
-    last = chunks - 1
+    group = 512 // span
+    last = chunks // group - 1
+    fold = 512 // cols
     shape = jax.ShapeDtypeStruct
+    fixed = lambda v: pl.BlockSpec(v.shape, lambda k: (0,) * v.ndim)
+    small = [stitched, d_stitch, d_bias]
     return pl.pallas_call(
         write_kernel,
-        grid=(nb,),
-        out_shape=[shape((1, per, nb * cols), F32), shape((towers, ktaps, cout), F32), shape((towers, cout), F32), shape((2, towers, cout), F32)],
-        in_specs=[pl.BlockSpec((live, per), lambda k: (0, 0)), pl.BlockSpec((1, live, cols), lambda k: (k, 0, 0)),
-                  pl.BlockSpec((towers, 1, cout, span), lambda k: (0, jnp.minimum(k, last), 0, 0))],
-        out_specs=[pl.BlockSpec((1, per, cols), lambda k: (0, 0, k)),
-                   pl.BlockSpec((towers, span, cout), lambda k: (0, jnp.minimum(k, last), 0)),
-                   pl.BlockSpec((towers, cout), lambda k: (0, 0)), pl.BlockSpec((2, towers, cout), lambda k: (0, 0, 0))],
-        compiler_params=pltpu.CompilerParams(vmem_limit_bytes=32 * 2**20),
-    )(f, g, dw)
+        grid=(nb // fold,),
+        out_shape=[shape((1, per, nb * cols), F32), shape((towers, ktaps, cout), F32), shape((towers, cout), F32),
+                   shape((2, towers, cout), F32)] + [shape(v.shape, v.dtype) for v in small],
+        in_specs=[pl.BlockSpec((per, live), lambda k: (0, 0)), pl.BlockSpec((fold, live, cols), lambda k: (k, 0, 0)),
+                  pl.BlockSpec((towers, group, cout, span), lambda k: (0, jnp.minimum(k, last), 0, 0))] + [fixed(v) for v in small],
+        out_specs=[pl.BlockSpec((1, per, fold * cols), lambda k: (0, 0, k)),
+                   pl.BlockSpec((towers, group * span, cout), lambda k: (0, jnp.minimum(k, last), 0)),
+                   pl.BlockSpec((towers, cout), lambda k: (0, 0)), pl.BlockSpec((2, towers, cout), lambda k: (0, 0, 0))] + [fixed(v) for v in small],
+        compiler_params=pltpu.CompilerParams(vmem_limit_bytes=60 * 2**20),
+    )(f, g, dw, *small)
 
 
 def shards(crop_pixels, live_rows, conv_weight, conv_bias, stitch_conv, fc_weight, fc_bias, stitch_fc, cotangent):
@@ -815,10 +799,11 @@
     cin, cout = conv_weight.shape[3:]
     live = slots * nb
     stitched, dx, f, dh, dw, d_stitch_fc, d_fc_bias = whole_layer(
-        live_rows, crop_pixels, conv_weight.reshape(2, 9 * cin, cout), conv_bias, stitch_conv, cotangent[0], fc_weight[0], fc_bias, stitch_fc, nb)
+        live_rows, crop_pixels.transpose(1, 2, 0, 3), conv_weight.reshape(2, 9 * cin, cout), conv_bias, stitch_conv, cotangent[0], fc_weight[0], fc_bias, stitch_fc, nb)
     dw = dw.reshape(2, dw.shape[1], cout, dw.shape[-1])
-    d_fc_weight, d_kernel, d_conv_bias, d_stitch_conv = write_grads(f, dh.reshape(nb, live, cols), dw, nb, cols, 9 * cin)
-    return stitched, dx, d_kernel.reshape(conv_weight.shape), d_conv_bias, d_stitch_conv, d_fc_weight, d_fc_bias, d_stitch_fc
+    d_fc_weight, d_kernel, d_conv_bias, d_stitch_conv, stitched, d_stitch_fc, d_fc_bias = write_grads(
+        f, dh.reshape(nb, live, cols), dw, stitched, d_stitch_fc, d_fc_bias, nb, cols, 9 * cin)
+    return stitched, dx.transpose(2, 0, 1, 3), d_kernel.reshape(conv_weight.shape), d_conv_bias, d_stitch_conv, d_fc_weight, d_fc_bias, d_stitch_fc
 
 
 def solution(mesh):

time: 199 us -> 187 us (0.940)
  local copies, waits for them, and re-layouts: 10.9 us -> 1.31 us
  Pallas kernels: 186 us -> 184 us
    unnamed x17 -> x3, local copies, waits for them, and re-layouts: 10.9 us -> 1.31 us
    pallas_call x1, Pallas kernels: 176 us -> 174 us  [whole_layer(): pl.pallas_call(functools.partial(whole_kernel, parts, per), out_shape=[sh...]
where the time goes in v5:
time: 187 us
  Pallas kernels  184 us (98%)
    pallas_call x1, Pallas kernels, whole_layer(): pl.pallas_call(functools.partial(whole_kernel, parts, per), out_shape=[sh...  174 us
    pallas_call x1, Pallas kernels, write_grads(): pl.pallas_call(write_kernel, grid=(nb // fold,), out_shape=[shape((1, per...  10.4 us

profile of v5, /device:TPU:1, one launch (start us, length us, event | category | flops | bytes accessed | tf_op | source)
XLA Modules:
  0.0 186.9 jit_solution(4413558971047341206)
XLA Ops:
  1.3 173.9 %shard_map.152 = (bf16[1,32,4096]{2,1,0:T(8,128)(2,1)}, bf16[13,13,16,384]{3,2,1,0:T(8,128)(2,1)}, bf16[576,256]{1,0:T(8,128)(2,1)}, bf16[4,2,2,256,256]{4,3,2,1...) custom-call(s32[1]{0:T(128)S(6)} %copy.18.live_ref, ...), custom_call_target="tpu_custom_call" | custom-call | tf_op jit(solution)/shard_map/pallas_call | solution.py:730
  175.2 0.0 copy-start
  175.2 10.4 %shard_map.153 = (f32[1,576,4096]{2,1,0:T(8,128)}, f32[2,3456,256]{2,1,0:T(8,128)}, f32[2,256]{1,0:T(2,128)}, f32[2,2,256]{2,1,0:T(2,128)}, bf16[1,32,4096]{2,1,...) custom-call(bf16[576,256]{1,0:T(8,128)(2,1)} %get-tuple-element.22.f_ref, bf16[16,256,256]{2,1,0:T(8,128)(2,1)} %bitcast.11, ...), custom_call_target="tpu_custom_call" | custom-call | tf_op jit(solution)/shard_map/pallas_call | solution.py:780
  185.5 0.0 copy-done
  185.5 1.3 copy.19
Async XLA Ops:
  175.2 10.4 %copy-start = (bf16[13,13,16,384]{3,2,1,0:T(8,128)(2,1)S(1)}, bf16[13,13,16,384]{3,2,1,0:T(8,128)(2,1)}, u32[]{:S(2)}) copy-start(bf16[13,13,16,384]{3,2,1,0:T(8,128)(2,1)} %get-tuple-element.29) | copy-start | bytes 6230020

commit v6 on v5

--- a/solution.py
+++ b/solution.py
@@ -510,7 +510,9 @@
     gate, cot, gate_other = gates[0].astype(F32), cots[0].astype(F32), gates[1].astype(F32)
     total_rows = [jnp.sum(cot * gate, axis=0, keepdims=True), jnp.sum(cot * gate_other, axis=0, keepdims=True),
                   jnp.sum(g[here[0], here[1], here[2]].astype(F32), axis=0, keepdims=True)]
-    wide[me] = jnp.concatenate(total_rows + [jnp.zeros((5, cols), F32)], axis=0)
+    fold = cols // 128
+    lines = [v[:, k * 128:(k + 1) * 128] for v in total_rows for k in range(fold)]
+    wide[me] = jnp.concatenate(lines + [jnp.zeros((8 - len(lines), 128), F32)], axis=0)
     def sums_copy(k):
         d = lax.rem(me + k, total)
         return pltpu.make_async_remote_copy(
@@ -556,11 +558,12 @@
         out_ref[0, :, k * cols:(k + 1) * cols] = sgot[k]
     lax.fori_loop(1, total, lambda k, _: (sums_copy(k).wait_recv(), 0)[1], 0)
     for k in range(nb):
-        at = slice(k * cols, (k + 1) * cols)
         for u in range(2):
-            stitch_ref[u, u:u + 1, at] = wide[2 * k + u, 0:1]
-            stitch_ref[u, 1 - u:2 - u, at] = wide[2 * k + u, 1:2]
-            fbias_ref[u:u + 1, at] = wide[2 * k + u, 2:3]
+            for j in range(fold):
+                at = slice(k * cols + j * 128, k * cols + (j + 1) * 128)
+                stitch_ref[u, u:u + 1, at] = wide[2 * k + u, j:j + 1]
+                stitch_ref[u, 1 - u:2 - u, at] = wide[2 * k + u, fold + j:fold + j + 1]
+                fbias_ref[u:u + 1, at] = wide[2 * k + u, 2 * fold + j:2 * fold + j + 1]
     lax.fori_loop(1, total, lambda k, _: (grad_copy(k).wait_recv(), 0)[1], 0)
 
     for u in range(towers):
@@ -632,23 +635,23 @@
             for n in range(chunks)]
     core, share_back = {}, {}
 
+    def tower(u):
+        return pl.ds(pl.multiple_of(u * cout, cout), cout)
+
     def compute(n):
-        win = window(n)
-        def half(u):
-            at = pl.ds(pl.multiple_of(u * cout, cout), cout)
-            v = jnp.dot(dt[at, :], win, preferred_element_type=F32)
-            if n == chunks - 1:
-                extra = sums_t[at, :]
-                lane = lax.broadcasted_iota(jnp.int32, extra.shape, 1)
-                v = jnp.concatenate([v[:, :span - 128], jnp.where(lane == 0, v[:, span - 128:], extra)], axis=1)
-            return v
-        give[n] = half(1 - t).astype(BF16)
+        slot = n % keep.shape[0]
+        v = jnp.dot(dt[...], window(n), preferred_element_type=F32)
+        if n == chunks - 1:
+            extra = sums_t[...]
+            lane = lax.broadcasted_iota(jnp.int32, extra.shape, 1)
+            v = jnp.concatenate([v[:, :span - 128], jnp.where(lane == 0, v[:, span - 128:], extra)], axis=1)
+        keep[slot] = v
+        give[n] = keep[slot, tower(1 - t)].astype(BF16)
         core[n] = send(give.at[n], take.at[n], hs.at[n, 0], hr.at[n, 0], other)
-        keep[n % keep.shape[0]] = half(t)
 
     def merge(n):
         core[n].wait_recv()
-        cs_[n] = (keep[n % keep.shape[0]] + take[n].astype(F32)).astype(BF16).reshape(cs_.shape[1:])
+        cs_[n] = (keep[n % keep.shape[0], tower(t)] + take[n].astype(F32)).astype(BF16).reshape(cs_.shape[1:])
         lots[n].send1()
 
     def finish(n):
@@ -741,9 +744,9 @@
             vm(nb, per, cols), vm(nb, 2 * slots, cols), vm(nb, 2 * slots, cols), vm(nb, 2 * slots, cols), vm(rows, live),
             vm(d0, d1, d2, live, cols), vm(n, d1 - 1, d0, d1, size, cols), vm(n, d0, d1, size, cols),
             vm(n, d1 - 1, d0, size, cols), vm(n, d0, size, cols), vm(n, d0 - 1, size, cols),
-            vm(2, live, cols), vm(2, live, cols), vf(total, 8, cols), vf(live, per),
+            vm(2, live, cols), vm(2, live, cols), vf(total, 8, 128), vf(live, per),
             vf(pool + 2, pool + 2, slots, wide), vm(side + 2, side + 2, slots, wide), vm(cells, slots, wide), vm(wide, cells * slots),
-            vf(2, cout, span), vm(chunks, d0, d1, d2, h, span), vm(chunks, d1 - 1, d0, d1, h, span), vm(chunks, d0, d1, h, span),
+            vf(2, wide, span), vm(chunks, d0, d1, d2, h, span), vm(chunks, d1 - 1, d0, d1, h, span), vm(chunks, d0, d1, h, span),
             vm(chunks, d1 - 1, d0, h, span), vm(chunks, d0, h, span), vm(chunks, d0 - 1, h, span), vf(wide, 128),
             dma(side), pltpu.SemaphoreType.DMA, dma(nb), dma(total), dma(total), dma(nb), dma(nb), dma(2), dma(2), dma(nb), dma(nb),
             dma(total), dma(total), dma(n, hops(nb)), dma(n, hops(nb)), dma(total), dma(total),
@@ -752,12 +755,12 @@
     )(live_rows, x, cw, cbias, cmix, cot, w, fbias, fmix)
 
 
-def write_kernel(f_ref, g_ref, dw_ref, st_ref, fs_ref, fb_ref, fc_ref, conv_ref, bias_ref, mix_ref, st_out, fs_out, fb_out):
+def write_kernel(pad, f_ref, g_ref, dw_ref, st_ref, fs_ref, fb_ref, fc_ref, conv_ref, bias_ref, mix_ref, st_out, fs_out, fb_out):
     cols = g_ref.shape[2]
     for i in range(g_ref.shape[0]):
         fc_ref[0, :, i * cols:(i + 1) * cols] = jnp.dot(f_ref[...], g_ref[i], preferred_element_type=F32)
     flat = [jnp.concatenate([dw_ref[u, k].T for k in range(dw_ref.shape[1])], axis=0).astype(F32) for u in range(dw_ref.shape[0])]
-    half = flat[0].shape[0] - 128
+    half = flat[0].shape[0] - 128 - pad
     for u, v in enumerate(flat):
         conv_ref[u] = v
         bias_ref[u:u + 1] = v[half:half + 1]
@@ -771,14 +774,14 @@
 def write_grads(f, g, dw, stitched, d_stitch, d_bias, nb, cols, ktaps):
     per, live = f.shape
     towers, chunks, cout, span = dw.shape
-    group = 512 // span
-    last = chunks // group - 1
-    fold = 512 // cols
+    group = 1024 // span
+    last = -(-chunks // group) - 1
+    fold = 1024 // cols
     shape = jax.ShapeDtypeStruct
     fixed = lambda v: pl.BlockSpec(v.shape, lambda k: (0,) * v.ndim)
     small = [stitched, d_stitch, d_bias]
     return pl.pallas_call(
-        write_kernel,
+        functools.partial(write_kernel, (last + 1) * group * span - chunks * span),
         grid=(nb // fold,),
         out_shape=[shape((1, per, nb * cols), F32), shape((towers, ktaps, cout), F32), shape((towers, cout), F32),
                    shape((2, towers, cout), F32)] + [shape(v.shape, v.dtype) for v in small],

time: 187 us -> 184 us (0.984)
  Pallas kernels: 184 us -> 181 us
where the time goes in v6:
time: 184 us; the launch traced here: 183 us
  Pallas kernels  181 us (98%)
    pallas_call x1, Pallas kernels, whole_layer(): pl.pallas_call(functools.partial(whole_kernel, parts, per), out_shape=[sh...  172 us
    pallas_call x1, Pallas kernels, write_grads(): pl.pallas_call(functools.partial(write_kernel, (last + 1) * group * span...  8.51 us

profile of v6, /device:TPU:1, one launch (start us, length us, event | category | flops | bytes accessed | tf_op | source)
XLA Modules:
  0.0 183.5 jit_solution(16675646737009281267)
XLA Ops:
  1.3 172.3 %shard_map.152 = (bf16[1,32,4096]{2,1,0:T(8,128)(2,1)}, bf16[13,13,16,384]{3,2,1,0:T(8,128)(2,1)}, bf16[576,256]{1,0:T(8,128)(2,1)}, bf16[4,2,2,256,256]{4,3,2,1...) custom-call(s32[1]{0:T(128)S(6)} %copy.18.live_ref, ...), custom_call_target="tpu_custom_call" | custom-call | tf_op jit(solution)/shard_map/pallas_call | solution.py:733
  173.6 0.0 copy-start
  173.6 8.5 %shard_map.153 = (f32[1,576,4096]{2,1,0:T(8,128)}, f32[2,3456,256]{2,1,0:T(8,128)}, f32[2,256]{1,0:T(2,128)}, f32[2,2,256]{2,1,0:T(2,128)}, bf16[1,32,4096]{2,1,...) custom-call(bf16[576,256]{1,0:T(8,128)(2,1)} %get-tuple-element.22.f_ref, bf16[16,256,256]{2,1,0:T(8,128)(2,1)} %bitcast.11, ...), custom_call_target="tpu_custom_call" | custom-call | tf_op jit(solution)/shard_map/pallas_call | solution.py:783
  182.2 0.0 copy-done
  182.2 1.3 copy.19
Async XLA Ops:
  173.6 8.5 %copy-start = (bf16[13,13,16,384]{3,2,1,0:T(8,128)(2,1)S(1)}, bf16[13,13,16,384]{3,2,1,0:T(8,128)(2,1)}, u32[]{:S(2)}) copy-start(bf16[13,13,16,384]{3,2,1,0:T(8,128)(2,1)} %get-tuple-element.29) | copy-start | bytes 6230020
